TPU v7x, 256 devices: a whole 4x4x8 slice. The times are simulated.
256 devices in a mesh: section: 16 (over z, core), expert: 16 (over x, y).
Axes of the slice: x: 4, y: 4, z: 8, core: 2. Of those that a mesh axis runs over, the one named last changes fastest.
Arguments:
- tokens: bfloat16 [2048, 3072], P('expert'), may hold values from -6 to 6
- norm_gain: float32 [3072], replicated, may hold values from 0.1 to 1.9
- expert_ids: int32 [2048, 4], P('expert'), may hold values from 0 to 15, all different within a row; in each aligned block of 128 rows (0 to 127, 128 to 255, ...) at most 64 rows name the same one
- gates: float32 [2048, 4], P('expert'), may hold values from 0.1 to 1
- gate_proj: bfloat16 [16, 3072, 8192], P('expert', None, 'section'), may hold values from -0.109375 to 0.109375
- up_proj: bfloat16 [16, 3072, 8192], P('expert', None, 'section'), may hold values from -0.109375 to 0.109375
- down_proj: bfloat16 [16, 8192, 3072], P('expert', 'section'), may hold values from -0.0625 to 0.0625
Outputs:
- mixed: bfloat16 [2048, 3072], P('expert')
Inputs may be any that keep to these rules, and one draw needn't show every extreme that they name: `expert_ids`: each token names 4 different experts; among the 128 tokens of one aligned block no expert is named more than 64 times, and in every draw some block names some expert exactly 64 times.
All inputs are finite; a program needn't handle non-finite values.
Results may differ from a plain program's by a relative error of at most 0.024.
Values may be sent and summed in bfloat16 or wider, within the bound.
A program may use at most 64 MiB of HBM per device.

v0:
```python
import jax
import jax.numpy as jnp
from jax import lax
from jax.sharding import PartitionSpec as P


def placement_matrix(block_ids, experts, capacity, expert_major):
    flattened = block_ids.reshape(-1)
    onehot = (flattened[:, None] == jnp.arange(experts, dtype=jnp.int32)[None, :]).astype(jnp.int32)
    slot_index = jnp.sum((jnp.cumsum(onehot, axis=0) - onehot) * onehot, axis=1)
    if expert_major:
        target = flattened * capacity + slot_index
    else:
        target = slot_index * experts + flattened
    return jnp.arange(experts * capacity, dtype=jnp.int32)[:, None] == target[None, :]


def expand_hidden(row_block, gate_weight, up_weight):
    gate_value = jnp.dot(row_block, gate_weight, preferred_element_type=jnp.float32)
    up_value = jnp.dot(row_block, up_weight, preferred_element_type=jnp.float32)
    return (jax.nn.silu(gate_value) * up_value).astype(jnp.bfloat16)


def on_device(tokens, norm_gain, expert_ids, gates, gate_proj, up_proj, down_proj):
    experts = lax.axis_size("expert")
    sections = lax.axis_size("section")
    tok_dev, top_count = expert_ids.shape
    capacity = min(tok_dev, 2 * tok_dev * top_count // experts)
    share_slots = capacity // sections
    features = tokens.shape[1]
    values = tokens.astype(jnp.float32)
    average = jnp.mean(values, axis=-1, keepdims=True)
    centered = values - average
    variance = jnp.mean(centered * centered, axis=-1, keepdims=True)
    normed = (centered * lax.rsqrt(variance + 1e-05) * norm_gain).astype(jnp.bfloat16)
    gate_weight = gate_proj[0]
    up_weight = up_proj[0]
    down_weight = down_proj[0]
    width = gate_weight.shape[1]
    select = placement_matrix(expert_ids, experts, capacity, True).astype(jnp.bfloat16)
    spread = jnp.repeat(normed, top_count, axis=0)
    packed = jnp.dot(select, spread, preferred_element_type=jnp.float32).astype(jnp.bfloat16)
    packed = packed.reshape(experts, capacity, features)
    received = lax.all_to_all(packed, "expert", split_axis=0, concat_axis=0, tiled=True)
    hidden = expand_hidden(received.reshape(-1, features), gate_weight, up_weight)
    hidden = hidden.reshape(experts, capacity, width)
    own_rows = share_slots * experts
    slot_count = own_rows * lax.axis_size("section") // experts
    part_rows = hidden
    part_rows = part_rows.transpose(1, 0, 2).reshape(slot_count * experts, width)
    summed = lax.psum_scatter(
        jnp.dot(part_rows, down_weight, preferred_element_type=jnp.float32).astype(jnp.bfloat16),
        "section",
        scatter_dimension=0,
        tiled=True,
    )
    expert_out = summed.reshape(share_slots, experts, features)
    returned = lax.all_to_all(expert_out, "expert", split_axis=1, concat_axis=1, tiled=True)
    all_slots = lax.all_gather(returned, "section", axis=0, tiled=True)
    chosen = placement_matrix(expert_ids, experts, capacity, False).astype(jnp.float32)
    pair_owner = jnp.arange(tok_dev * top_count, dtype=jnp.int32) // top_count
    owners = (pair_owner[None, :] == jnp.arange(tok_dev, dtype=jnp.int32)[:, None]).astype(
        jnp.float32
    )
    owners = owners * gates.reshape(-1)[None, :]
    combine = jnp.dot(owners, chosen.T, precision=lax.Precision.HIGHEST)
    mixed_rows = jnp.dot(
        combine,
        all_slots.reshape(-1, features).astype(jnp.float32),
        precision=lax.Precision.HIGHEST,
    )
    return mixed_rows.astype(jnp.bfloat16)


def solution(mesh):
    return jax.shard_map(
        on_device,
        mesh=mesh,
        in_specs=(
            P("expert", None),
            P(),
            P("expert", None),
            P("expert", None),
            P("expert", None, "section"),
            P("expert", None, "section"),
            P("expert", "section", None),
        ),
        out_specs=P("expert", None),
        check_vma=False,
    )
```

profile of v0, /device:TPU:1, one launch (start us, length us, event | category | flops | bytes accessed | tf_op | source)
XLA Modules:
  0.0 262.4 jit_solution(12200895628553274673)
XLA Ops:
  6.5 0.0 copy-start
  6.5 0.0 reduce-scatter.2.cloned.1.call-start
  6.5 0.9 copy.14
  7.5 0.1 eq.79
  7.6 0.1 eq.75
  7.7 1.2 reduce-window.6
  8.9 0.2 slice_reduce_fusion
  9.1 0.1 fusion.21
  9.2 1.3 convert_reduce_fusion
  10.6 1.5 fusion.10
  12.1 1.5 fusion.12
  13.5 2.6 broadcast_in_dim.2
  16.1 5.9 %reshape.84 = bf16[512,3072]{1,0:T(8,128)(2,1)} reshape(bf16[128,4,3072]{2,1,0:T(4,128)(2,1)} %broadcast_in_dim.2) | data formatting | bytes 6291456 | tf_op jit(solution)/shard_map/reshape | solution.py:41
  22.0 5.5 %convolution_convert_fusion.1 = bf16[1024,3072]{1,0:T(8,128)(2,1)S(1)} fusion(bf16[512,3072]{1,0:T(8,128)(2,1)} %reshape.84, s32[512]{0:T(512)S(1)} %get-tuple-element.5), kind=kOutput, calls=%fused_computation.1 | convolution fusion | flops 3224895488 | bytes 9439232 | tf_op jit(solution)/shard_map/dot_general | solution.py:42
  27.5 0.0 copy-start.2
  27.6 79.6 %all_to_all.10 = bf16[16,64,3072]{2,1,0:T(8,128)(2,1)S(1)} all-to-all(bf16[16,64,3072]{2,1,0:T(8,128)(2,1)S(1)} %bitcast.44), channel_id=1, replica_groups=mesh['section'=16,'expert'=16] {'expert'}, dimensions={0} | all-to-all | bytes 12582912 | tf_op jit(solution)/shard_map/all_to_all | solution.py:44
  107.2 0.0 copy-done.2
  107.2 0.0 copy-start.3
  107.2 3.4 %fusion.1 = f32[1024,512]{1,0:T(8,128)S(1)} fusion(bf16[1024,3072]{1,0:T(8,128)(2,1)S(1)} %bitcast.45, bf16[1,3072,512]{2,1,0:T(8,128)(2,1)S(1)} %copy-done.2), kind=kOutput, calls=%fused_computation.4 | convolution fusion | flops 3221225472 | bytes 11534336 | tf_op jit(solution)/shard_map/dot_general | solution.py:20
  110.6 0.0 copy-done.3
  110.6 3.7 %multiply_convert_fusion = bf16[1024,512]{1,0:T(8,128)(2,1)S(1)} fusion(f32[1024,512]{1,0:T(8,128)S(1)} %fusion.1, bf16[1024,3072]{1,0:T(8,128)(2,1)S(1)} %bitcast.46, bf16[1,3072,512]{2,1,0:T(8,128)(2,1)S(1)} %copy-done.3), kind=kOutput, calls=%fused_computation.8 | convolution fusion | flops 3224371200 | bytes 12582912 | tf_op jit(solution)/shard_map/dot_general | solution.py:19
  114.3 0.6 copy.17
  114.9 0.0 copy-done
  114.9 5.3 %convolution_convert_fusion = bf16[1024,3072]{1,0:T(8,128)(2,1)} fusion(bf16[1024,512]{1,0:T(8,128)(2,1)S(1)} %bitcast.49, bf16[1,512,3072]{2,1,0:T(8,128)(2,1)S(1)} %copy-done), kind=kOutput, calls=%fused_computation | convolution fusion | flops 3224371200 | bytes 10485760 | tf_op jit(solution)/shard_map/dot_general | solution.py:52
  120.3 0.0 copy-start.1
  120.3 0.0 reduce-scatter.2.cloned.1.call-update
  120.3 0.0 all-gather.2.cloned.1.call-start
  120.3 65.6 %reduce-scatter.2.cloned.1.call-done = bf16[64,3072]{1,0:T(8,128)(2,1)} async-done(((bf16[1024,3072]{1,0:T(8,128)(2,1)}), bf16[64,3072]{1,0:T(8,128)(2,1)}) %reduce-scatter.2.cloned.1.call-update) | async-done | bytes 393232 | tf_op jit(solution)/shard_map/reduce_scatter | solution.py:51
  185.9 1.3 copy.18
  187.2 14.3 %all_to_all.11 = bf16[4,16,3072]{2,0,1:T(4,128)(2,1)S(1)} all-to-all(bf16[4,16,3072]{2,0,1:T(4,128)(2,1)S(1)} %copy.18), channel_id=1, replica_groups=mesh['section'=16,'expert'=16] {'expert'}, dimensions={1} | all-to-all | bytes 786432 | tf_op jit(solution)/shard_map/all_to_all | solution.py:58
  201.5 0.9 copy.19
  202.4 0.0 all-gather.2.cloned.1.call-update
  202.4 0.0 copy-done.1
  202.4 0.1 copy.13
  202.5 0.1 mul.60
  202.6 2.1 fusion.5
  204.7 44.4 %all-gather.2.cloned.1.call-done = bf16[64,16,3072]{2,1,0:T(8,128)(2,1)} async-done(((bf16[4,16,3072]{2,1,0:T(8,128)(2,1)}), bf16[64,16,3072]{2,1,0:T(8,128)(2,1)}) %all-gather.2.cloned.1.call-update) | async-done | bytes 6291472 | tf_op jit(solution)/shard_map/all_gather | solution.py:59
  249.1 6.5 %convolution_convert_fusion.2 = bf16[128,3072]{1,0:T(8,128)(2,1)} fusion(f32[128,1024]{1,0:T(8,128)} %fusion.5, bf16[1024,3072]{1,0:T(8,128)(2,1)} %bitcast.47), kind=kOutput, calls=%fused_computation.2 | convolution fusion | flops 4832231424 | bytes 7602176 | tf_op jit(solution)/shard_map/dot_general | solution.py:67
  (7 shorter events, 0.1 us)
Async XLA Ops:
  6.5 108.4 %copy-start = (bf16[1,512,3072]{2,1,0:T(8,128)(2,1)S(1)}, bf16[1,512,3072]{2,1,0:T(8,128)(2,1)}, u32[]{:S(2)}) copy-start(bf16[1,512,3072]{2,1,0:T(8,128)(2,1)} %param.13) | copy-start | bytes 9437188
  6.5 179.4 %reduce-scatter.2.cloned.1.call-start = ((), (), s32[]{:S(2)}) async-start(), calls=%async_computation.3 | async-start | bytes 6684672 | tf_op jit(solution)/shard_map/reduce_scatter | solution.py:51
  27.5 79.6 %copy-start.2 = (bf16[1,3072,512]{2,1,0:T(8,128)(2,1)S(1)}, bf16[1,3072,512]{2,1,0:T(8,128)(2,1)}, u32[]{:S(2)}) copy-start(bf16[1,3072,512]{2,1,0:T(8,128)(2,1)} %param.12) | copy-start | bytes 9437188
  107.2 3.4 %copy-start.3 = (bf16[1,3072,512]{2,1,0:T(8,128)(2,1)S(1)}, bf16[1,3072,512]{2,1,0:T(8,128)(2,1)}, u32[]{:S(2)}) copy-start(bf16[1,3072,512]{2,1,0:T(8,128)(2,1)} %param.11) | copy-start | bytes 9437188
  120.3 82.1 %copy-start.1 = (f32[128,4]{0,1:T(4,128)S(1)}, f32[128,4]{0,1:T(4,128)}, u32[]{:S(2)}) copy-start(f32[128,4]{0,1:T(4,128)} %param.10) | copy-start | bytes 6148
  120.3 128.8 %all-gather.2.cloned.1.call-start = ((), (), s32[]{:S(2)}) async-start(), calls=%async_computation.4 | async-start | bytes 6684672 | tf_op jit(solution)/shard_map/all_gather | solution.py:59
Sparse Core Ops, SparseCore 0:
  120.4 65.4 reduce-scatter.1
  202.5 46.5 all-gather.1
where the time goes:
time: 263 us; the launch traced here: 262 us
  waiting for transfers between devices  110 us (42%)
  blocking collectives  93.9 us (36%)
  matrix products  26.6 us (10%)
  between operations  13.5 us (5%)
  local copies, waits for them, and re-layouts  12.9 us (5%)
  other arithmetic  5.59 us (2%)
    all_to_all x1, blocking collectives, on_device(): lax.all_to_all(packed, 'expert', split_axis=0, concat_axis=0, tiled=True)  79.6 us
    reduce_scatter x1, waiting for transfers between devices, on_device(): lax.psum_scatter(jnp.dot(part_rows, down_weight, preferred_element_type=j...  65.6 us
    all_gather x1, waiting for transfers between devices, on_device(): all_slots = lax.all_gather(returned, 'section', axis=0, tiled=True)  44.4 us
    all_to_all x1, blocking collectives, on_device(): lax.all_to_all(expert_out, 'expert', split_axis=1, concat_axis=1, tiled=T...  14.3 us
    dot_general x1, matrix products, on_device(): jnp.dot(combine, all_slots.reshape(-1, features).astype(jnp.float32), pre...  6.5 us
    reshape x1, local copies, waits for them, and re-layouts, on_device(): spread = jnp.repeat(normed, top_count, axis=0)  5.89 us
    dot_general x1, matrix products, on_device(): jnp.dot(select, spread, preferred_element_type=jnp.float32)  5.51 us
    dot_general x1, matrix products, on_device(): jnp.dot(part_rows, down_weight, preferred_element_type=jnp.float32)  5.34 us
  transfers between devices with their start and end apart: 2, of which 2 were waited for; matrix products, arithmetic and copies ran while one was open for 1% of the time, Pallas kernels for 0%

commit v1 on v0

v1 whole, which is shorter than its diff:
```python
import functools

import jax
import jax.numpy as jnp
from jax import lax
from jax.experimental import pallas as pl
from jax.experimental.pallas import tpu as pltpu
from jax.sharding import PartitionSpec as P

MESH = pl.DeviceIdType.MESH
BATCHES = 4
SLOTS = 16
NZ = 8
SIDE = 4
XY = [(dx, dy) for dx in range(SIDE) for dy in range(SIDE) if (dx, dy) != (0, 0)]
ORDER = (4, 3, 5, 2, 6, 1, 7, 0)
BF = jnp.bfloat16
F32 = jnp.float32


def kernel(
    tok, gain, ids, gates, wg_hbm, wu_hbm, wd_hbm, out,
    wg, wu, wd, normed, sel, chi, clo, packed, xin, gacc, uacc, part, sib,
    asend, arecv, bsend, brecv, ret_out, ret, acc, mixed,
    w_sem, xs, xr, fs, fr, ps, pr, as_, ar, bs, br, rs, rr, os_, or_, gs, gr,
):
    sec, me = lax.axis_index("section"), lax.axis_index("expert")
    z, c = sec // 2, sec % 2
    x, y = me // SIDE, me % SIDE
    experts = SIDE * SIDE
    half = normed.shape[2]
    width = wg.shape[2]
    chunk = wd.shape[2]
    rows = experts * SLOTS
    hrows = rows // 2
    sigma = 1 - 2 * c

    def zdev(dz, cc):
        return (lax.rem(z + dz + 2 * NZ, NZ) * 2 + cc, me)

    def xydev(dx, dy):
        return lax.rem(x + dx, SIDE) * SIDE + lax.rem(y + dy, SIDE)

    def rel(k):
        return lax.rem(k + 2 * NZ, NZ)

    sibling = (z * 2 + 1 - c, me)

    barrier = pltpu.get_barrier_semaphore()
    for dx, dy in XY:
        pl.semaphore_signal(barrier, inc=1, device_id=(sec, xydev(dx, dy)), device_id_type=MESH)
    pl.semaphore_signal(barrier, inc=1, device_id=sibling, device_id_type=MESH)
    for k in range(1, NZ):
        pl.semaphore_signal(barrier, inc=1, device_id=zdev(k, c), device_id_type=MESH)

    loads = []
    for h in range(2):
        first = pl.ds(pl.multiple_of(half * lax.rem(c + h, 2), half), half)
        loads.append(pltpu.make_async_copy(wg_hbm.at[0, first, :], wg.at[h], w_sem.at[2 * h]))
        loads.append(pltpu.make_async_copy(wu_hbm.at[0, first, :], wu.at[h], w_sem.at[2 * h + 1]))
    down_loads = []
    for k in range(NZ):
        cols = pl.ds(pl.multiple_of(chunk * rel(z + k), chunk), chunk)
        down_loads.append(pltpu.make_async_copy(wd_hbm.at[0, :, cols], wd.at[k], w_sem.at[4 + k]))
    for load in loads + down_loads:
        load.start()

    values = tok[...].astype(F32)
    average = jnp.mean(values, axis=-1, keepdims=True)
    centered = values - average
    variance = jnp.mean(centered * centered, axis=-1, keepdims=True)
    result = (centered * lax.rsqrt(variance + 1e-05) * gain[...]).astype(BF)
    normed[0] = result[:, :half]
    normed[1] = result[:, half:]

    toks = tok.shape[0]
    e_iota = lax.broadcasted_iota(jnp.int32, (experts, toks), 0)
    named = jnp.zeros((experts, toks), jnp.bool_)
    weight = jnp.zeros((experts, toks), F32)
    for k in range(ids.shape[0]):
        hit = e_iota == ids[k : k + 1, :]
        named = named | hit
        weight = weight + jnp.where(hit, gates[k : k + 1, :], 0.0)
    earlier = lax.broadcasted_iota(jnp.int32, (toks, toks), 0) < lax.broadcasted_iota(jnp.int32, (toks, toks), 1)
    named_f = jnp.where(named, 1.0, 0.0)
    slot = jnp.dot(named_f.astype(BF), jnp.where(earlier, 1.0, 0.0).astype(BF), preferred_element_type=F32)
    slot = jnp.where(named, slot, -1.0)
    s_iota = lax.broadcasted_iota(jnp.int32, (SLOTS, toks), 0).astype(F32)
    for j in range(BATCHES):
        for e in range(experts):
            here = (slot[e : e + 1, :] - float(SLOTS * j)) == s_iota
            lines = pl.ds(SLOTS * e, SLOTS)
            sel[j, lines, :] = jnp.where(here, 1.0, 0.0).astype(BF)
            share = jnp.where(here, weight[e : e + 1, :], 0.0)
            top = share.astype(BF)
            chi[j, lines, :] = top
            clo[j, lines, :] = (share - top.astype(F32)).astype(BF)

    mine = pl.ds(pl.multiple_of(SLOTS * me, SLOTS), SLOTS)

    def pack(j):
        packed[j] = jnp.dot(sel[j], normed[c], preferred_element_type=F32).astype(BF)
        xin[j, 0, mine, :] = packed[j, mine, :]

    def dispatch(j):
        copies = []
        for o, (dx, dy) in enumerate(XY):
            to = xydev(dx, dy)
            src = pl.ds(pl.multiple_of(SLOTS * to, SLOTS), SLOTS)
            copies.append(pltpu.make_async_remote_copy(
                src_ref=packed.at[j, src, :], dst_ref=xin.at[j, 0, mine, :],
                send_sem=xs.at[j, o], recv_sem=xr.at[j, o],
                device_id=(sec, to), device_id_type=MESH))
        return copies

    sent = []

    def start(copies):
        for copy in copies:
            copy.start()
            sent.append(copy)
        return copies

    pack(0)
    pl.semaphore_wait(barrier, len(XY) + NZ)
    arrivals = {0: start(dispatch(0))}
    pack(1)
    arrivals[1] = start(dispatch(1))
    pack(2)
    pack(3)

    def sib_x(j):
        return pltpu.make_async_remote_copy(
            src_ref=xin.at[j, 0], dst_ref=xin.at[j, 1], send_sem=fs.at[j], recv_sem=fr.at[j],
            device_id=sibling, device_id_type=MESH)

    own_rows = pl.ds(pl.multiple_of(hrows * c, hrows), hrows)
    sib_rows = pl.ds(pl.multiple_of(hrows * (1 - c), hrows), hrows)

    def sib_p(j, k):
        return pltpu.make_async_remote_copy(
            src_ref=part.at[j, k, sib_rows, :], dst_ref=sib.at[j, k], send_sem=ps.at[j, k], recv_sem=pr.at[j, k],
            device_id=sibling, device_id_type=MESH)

    def chain_a(j, t):
        return pltpu.make_async_remote_copy(
            src_ref=asend.at[j, t], dst_ref=arecv.at[j, t], send_sem=as_.at[j, t], recv_sem=ar.at[j, t],
            device_id=zdev(-sigma, c), device_id_type=MESH)

    def chain_b(j, t):
        return pltpu.make_async_remote_copy(
            src_ref=bsend.at[j, t], dst_ref=brecv.at[j, t], send_sem=bs.at[j, t], recv_sem=br.at[j, t],
            device_id=zdev(sigma, c), device_id_type=MESH)

    def own_sum(j, k):
        return part[j, k, own_rows, :].astype(F32) + sib[j, k].astype(F32)

    def rs_step(j, t):
        if j < 0 or j >= BATCHES:
            return
        ka, kb = rel(4 + sigma * t), rel(4 - sigma * (1 + t))
        if t == 0:
            for k in ORDER:
                sib_p(j, k).wait_recv()
        total = own_sum(j, ka)
        if t > 0:
            chain_a(j, t - 1).wait_recv()
            total = total + arecv[j, t - 1].astype(F32)
        asend[j, t] = total.astype(BF)
        start([chain_a(j, t)])
        if t < 3:
            total = own_sum(j, kb)
            if t > 0:
                chain_b(j, t - 1).wait_recv()
                total = total + brecv[j, t - 1].astype(F32)
            bsend[j, t] = total.astype(BF)
            start([chain_b(j, t)])

    def back(j, i):
        b = c * (experts // 2) + i
        return b, pltpu.make_async_remote_copy(
            src_ref=ret_out.at[j, pl.ds(SLOTS * i, SLOTS), :], dst_ref=ret.at[j, mine, :],
            send_sem=rs.at[j, i], recv_sem=rr.at[j, me], device_id=(sec, b), device_id_type=MESH)

    def rs_final(j):
        if j < 0 or j >= BATCHES:
            return
        chain_a(j, 3).wait_recv()
        chain_b(j, 2).wait_recv()
        total = own_sum(j, 0) + arecv[j, 3].astype(F32) + brecv[j, 2].astype(F32)
        ret_out[j] = total.astype(BF)
        for i in range(experts // 2):
            b, copy = back(j, i)

            @pl.when(b != me)
            def _():
                copy.start()

            @pl.when(b == me)
            def _():
                ret[j, mine, :] = ret_out[j, pl.ds(SLOTS * i, SLOTS), :]

    home = c == me // (experts // 2)

    def mix(j):
        if j < 0 or j >= BATCHES:
            return

        @pl.when(home)
        def _():
            for e in range(experts):
                @pl.when(e != me)
                def _():
                    lines = pl.ds(SLOTS * e, SLOTS)
                    pltpu.make_async_remote_copy(
                        src_ref=ret_out.at[j, pl.ds(0, SLOTS), :], dst_ref=ret.at[j, lines, :],
                        send_sem=rs.at[j, 0], recv_sem=rr.at[j, e],
                        device_id=sibling, device_id_type=MESH).wait_recv()
            dims = (((0,), (0,)), ((), ()))
            term = lax.dot_general(chi[j], ret[j], dims, preferred_element_type=F32)
            term = term + lax.dot_general(clo[j], ret[j], dims, preferred_element_type=F32)
            acc[...] = term if j == 0 else acc[...] + term

    def take(j):
        for copy in arrivals[j]:
            copy.wait_recv()
        if j + 2 < BATCHES:
            arrivals[j + 2] = start(dispatch(j + 2))
        start([sib_x(j)])

    def up(j, h):
        gate = jnp.dot(xin[j, h], wg[h], preferred_element_type=F32)
        raised = jnp.dot(xin[j, h], wu[h], preferred_element_type=F32)
        if h == 0:
            gacc[...] = gate
            uacc[...] = raised
            return None
        gate = gacc[...] + gate
        raised = uacc[...] + raised
        return (gate / (1.0 + jnp.exp(-gate)) * raised).astype(BF)

    def down(j, hidden):
        for k in ORDER:
            part[j, k] = jnp.dot(hidden, wd[k], preferred_element_type=F32).astype(BF)
            start([sib_p(j, k)])

    for j in range(BATCHES):
        rs_step(j - 1, 1)
        rs_step(j - 2, 3)
        take(j)
        if j == 0:
            loads[0].wait()
            loads[1].wait()
        up(j, 0)
        if j == 0:
            loads[2].wait()
            loads[3].wait()
        sib_x(j).wait_recv()
        hidden = up(j, 1)
        rs_step(j - 1, 2)
        rs_final(j - 2)
        if j == 0:
            for load in down_loads:
                load.wait()
        down(j, hidden)
        rs_step(j, 0)
        mix(j - 3)
    last = BATCHES - 1
    rs_step(last, 1)
    rs_step(last - 1, 3)
    rs_step(last, 2)
    rs_final(last - 1)
    mix(last - 2)
    rs_step(last, 3)
    mix(last - 1)
    rs_final(last)
    mix(last)

    def give(k):
        return pltpu.make_async_remote_copy(
            src_ref=mixed.at[z], dst_ref=mixed.at[z], send_sem=os_.at[k], recv_sem=or_.at[k],
            device_id=zdev(k, c), device_id_type=MESH)

    def hand(k):
        at = rel(z + k)
        return pltpu.make_async_remote_copy(
            src_ref=mixed.at[at], dst_ref=mixed.at[at], send_sem=gs.at[k], recv_sem=gr.at[k],
            device_id=sibling, device_id_type=MESH)

    @pl.when(home)
    def _():
        mixed[z] = acc[...].astype(BF)
        for k in (1, 7, 2, 6, 3, 5, 4):
            give(k).start()
        hand(0).start()
        for k in (1, 7, 2, 6, 3, 5, 4):
            give(k).wait_recv()
            hand(NZ - k).start()
        for k in range(1, NZ):
            give(k).wait_send()
        for k in range(NZ):
            hand(k).wait_send()

    @pl.when(jnp.logical_not(home))
    def _():
        for k in range(NZ):
            hand(k).wait_recv()

    for k in range(NZ):
        out[:, chunk * k : chunk * (k + 1)] = mixed[k]
    for copy in sent:
        copy.wait_send()
    for j in range(BATCHES):
        for i in range(experts // 2):
            b, copy = back(j, i)

            @pl.when(b != me)
            def _():
                copy.wait_send()


def on_device(tokens, norm_gain, expert_ids, gates, gate_proj, up_proj, down_proj):
    toks, features = tokens.shape
    experts = lax.axis_size("expert")
    width = gate_proj.shape[2]
    half, chunk = features // 2, features // NZ
    rows = experts * SLOTS
    dma = pltpu.SemaphoreType.DMA
    vmem = pl.BlockSpec(memory_space=pltpu.VMEM)
    hbm = pl.BlockSpec(memory_space=pl.ANY)
    b = BATCHES
    scratch = [
        pltpu.VMEM((2, half, width), BF),
        pltpu.VMEM((2, half, width), BF),
        pltpu.VMEM((NZ, width, chunk), BF),
        pltpu.VMEM((2, toks, half), BF),
        pltpu.VMEM((b, rows, toks), BF),
        pltpu.VMEM((b, rows, toks), BF),
        pltpu.VMEM((b, rows, toks), BF),
        pltpu.VMEM((b, rows, half), BF),
        pltpu.VMEM((b, 2, rows, half), BF),
        pltpu.VMEM((rows, width), F32),
        pltpu.VMEM((rows, width), F32),
        pltpu.VMEM((b, NZ, rows, chunk), BF),
        pltpu.VMEM((b, NZ, rows // 2, chunk), BF),
        pltpu.VMEM((b, 4, rows // 2, chunk), BF),
        pltpu.VMEM((b, 4, rows // 2, chunk), BF),
        pltpu.VMEM((b, 3, rows // 2, chunk), BF),
        pltpu.VMEM((b, 3, rows // 2, chunk), BF),
        pltpu.VMEM((b, rows // 2, chunk), BF),
        pltpu.VMEM((b, rows, chunk), BF),
        pltpu.VMEM((toks, chunk), F32),
        pltpu.VMEM((NZ, toks, chunk), BF),
        dma((4 + NZ,)),
        dma((b, len(XY))), dma((b, len(XY))),
        dma((b,)), dma((b,)),
        dma((b, NZ)), dma((b, NZ)),
        dma((b, 4)), dma((b, 4)),
        dma((b, 3)), dma((b, 3)),
        dma((b, experts // 2)), dma((b, experts)),
        dma((NZ,)), dma((NZ,)),
        dma((NZ,)), dma((NZ,)),
    ]
    return pl.pallas_call(
        kernel,
        out_shape=jax.ShapeDtypeStruct((toks, features), BF),
        in_specs=[vmem, vmem, vmem, vmem, hbm, hbm, hbm],
        out_specs=vmem,
        scratch_shapes=scratch,
        compiler_params=pltpu.CompilerParams(
            collective_id=0, has_side_effects=True, vmem_limit_bytes=60 << 20
        ),
    )(tokens, norm_gain.reshape(1, -1), expert_ids.T, gates.T, gate_proj, up_proj, down_proj)


def solution(mesh):
    return jax.shard_map(
        on_device,
        mesh=mesh,
        in_specs=(
            P("expert", None),
            P(),
            P("expert", None),
            P("expert", None),
            P("expert", None, "section"),
            P("expert", None, "section"),
            P("expert", "section", None),
        ),
        out_specs=P("expert", None),
        check_vma=False,
    )
```

time: 263 us -> 114 us (0.43)
  Pallas kernels: 0 us -> 111 us
  waiting for transfers between devices: 110 us -> 0 us
  blocking collectives: 93.9 us -> 0 us
  matrix products: 26.6 us -> 0 us
  between operations: 13.5 us -> 0.01 us
  local copies, waits for them, and re-layouts: 12.9 us -> 2.06 us
  other arithmetic: 5.59 us -> 0 us
    pallas_call x0 -> x1, Pallas kernels: none -> 111 us  [on_device(): pl.pallas_call(kernel, out_shape=jax.ShapeDtypeStruct((toks, features), B...]
    all_to_all x2 -> x0, blocking collectives: 93.9 us -> none  [the longest x1 79.6 us: on_device(): lax.all_to_all(packed, 'expert', split_axis=0, concat_axis=0, tiled=True)]
    reduce_scatter x1 -> x0, waiting for transfers between devices: 65.6 us -> none  [on_device(): lax.psum_scatter(jnp.dot(part_rows, down_weight, preferred_element_type=j...]
    all_gather x1 -> x0, waiting for transfers between devices: 44.4 us -> none  [on_device(): all_slots = lax.all_gather(returned, 'section', axis=0, tiled=True)]
    dot_general x6 -> x0, matrix products: 26.6 us -> none  [the longest x1 6.5 us: on_device(): jnp.dot(combine, all_slots.reshape(-1, features).astype(jnp.float32), pre...]
    reshape x3 -> x0, local copies, waits for them, and re-layouts: 7.77 us -> none  [the longest x1 5.89 us: on_device(): spread = jnp.repeat(normed, top_count, axis=0)]
    reduce_sum x3 -> x0, other arithmetic: 2.91 us -> none  [the longest x1 1.49 us: on_device(): variance = jnp.mean(centered * centered, axis=-1, keepdims=True)]
  transfers between devices with their start and end apart: 2 -> 0, of which waited for: 2 -> 0; matrix products, arithmetic and copies ran while one was open for 1% -> 0% of each run, Pallas kernels for 0% -> 0%
where the time goes in v1:
time: 114 us; the launch traced here: 113 us
  Pallas kernels  111 us (97%)
  local copies, waits for them, and re-layouts  2.06 us (2%)
    pallas_call x1, Pallas kernels, on_device(): pl.pallas_call(kernel, out_shape=jax.ShapeDtypeStruct((toks, features), B...  111 us

profile of v1, /device:TPU:1, one launch (start us, length us, event | category | flops | bytes accessed | tf_op | source)
XLA Modules:
  0.0 113.4 jit_solution(4874805365653820879)
XLA Ops:
  0.0 111.4 %shard_map.73 = bf16[128,3072]{1,0:T(8,128)(2,1)} custom-call(bf16[128,3072]{1,0:T(8,128)(2,1)} %tok.1, f32[1,3072]{1,0:T(1,128)} %bitcast.3, s32[4,128]{1,0:T(4,128)} %bitcast.4, f32[4,128]{1,0:T(4,128)} %bitcast.5, bf16[1,3072,512]{2,1,0:T(8,128)(2,1)} %wg_hbm.1, bf16[1,3072,512]{2,1,0:T(8,128)(2,1)} %wu_hbm.1, bf16[1,512,3072]{2,1,0:T(8,128)(2,1)} %wd_hbm.1), custom_call_target="tpu_custom_call" | custom-call | tf_op jit(solution)/shard_map/pallas_call | solution.py:364
  111.4 2.1 %copy.9 = bf16[128,3072]{1,0:T(8,128)(2,1)} copy(bf16[128,3072]{1,0:T(8,128)(2,1)} %shard_map.73) | data formatting | bytes 1572864

commit v2 on v0

v2 whole, which is shorter than its diff:
```python
import jax
import jax.numpy as jnp
from jax import lax
from jax.experimental import pallas as pl
from jax.experimental.pallas import tpu as pltpu
from jax.sharding import PartitionSpec as P

MESH = pl.DeviceIdType.MESH
BATCHES = 4
ALONE = 2
SLOTS = 16
NZ = 8
SIDE = 4
XY = [(dx, dy) for dx in range(SIDE) for dy in range(SIDE) if (dx, dy) != (0, 0)]
ORDER = ((4, 3, 5, 2), (6, 1, 7, 0))
PLACE = {k: (g, i) for g, ks in enumerate(ORDER) for i, k in enumerate(ks)}
PIECES = 3
BF = jnp.bfloat16
F32 = jnp.float32


def kernel(
    tok, gain, ids, gates, wg_hbm, wu_hbm, wd_hbm, out,
    wg, wu, wd, line, slots, chi, clo, chi2, clo2, packed, xin, gacc, uacc, part, sib,
    asend, arecv, bsend, brecv, asend2, arecv2, bsend2, brecv2, ret_out, ret, ret_out2, ret2, acc, mixed,
    w_sem, ls, lr, ns, nr, xs, xr, fs, fr, ps, pr, as_, ar, bs, br, as2, ar2, bs2, br2, rs, rr, rr2, os_, or_, gs, gr,
):
    sec, me = lax.axis_index("section"), lax.axis_index("expert")
    z, c = sec // 2, sec % 2
    x, y = me // SIDE, me % SIDE
    experts = SIDE * SIDE
    blocks = experts // 2
    toks = tok.shape[0]
    htoks = toks // 2
    fine = line.shape[3]
    half = fine * PIECES
    col = mixed.shape[3]
    chunk = col * PIECES
    hrows = blocks * SLOTS
    late = BATCHES - ALONE
    first_step, then_step = SIDE * (1 - c) + c, SIDE * c + (1 - c)
    first_at, then_at = x * (1 - c) + y * c, y * (1 - c) + x * c

    def on_first(i):
        return me + (i - first_at) * first_step

    def on_then(i):
        return me + (i - then_at) * then_step

    def zdev(dz):
        return (lax.rem(z + dz + 2 * NZ, NZ) * 2 + c, me)

    def xydev(dx, dy):
        return lax.rem(x + dx, SIDE) * SIDE + lax.rem(y + dy, SIDE)

    other = z * 2 + 1 - c
    sibling = (other, me)

    barrier = pltpu.get_barrier_semaphore()
    for dx, dy in XY:
        for s in (sec, other):
            pl.semaphore_signal(barrier, inc=1, device_id=(s, xydev(dx, dy)), device_id_type=MESH)
    pl.semaphore_signal(barrier, inc=1, device_id=sibling, device_id_type=MESH)
    for k in range(1, NZ):
        pl.semaphore_signal(barrier, inc=1, device_id=zdev(k), device_id_type=MESH)

    loads = []
    for h in range(2):
        lines = pl.ds(pl.multiple_of(half * lax.rem(c + h, 2), half), half)
        loads.append(pltpu.make_async_copy(wg_hbm.at[0, lines, :], wg.at[h], w_sem.at[2 * h]))
        loads.append(pltpu.make_async_copy(wu_hbm.at[0, lines, :], wu.at[h], w_sem.at[2 * h + 1]))
    for load in loads:
        load.start()
    for k in range(NZ):
        cols = pl.ds(pl.multiple_of(chunk * lax.rem(z + k, NZ), chunk), chunk)
        g, i = PLACE[k]
        pltpu.make_async_copy(wd_hbm.at[0, :, cols], wd.at[g, :, pl.ds(chunk * i, chunk)], w_sem.at[4]).start()

    def await_bytes(ref, sem):
        pltpu.make_async_copy(ref, ref, sem).wait()

    e_iota = lax.broadcasted_iota(jnp.int32, (experts, toks), 0)
    named = jnp.zeros((experts, toks), jnp.bool_)
    weight = jnp.zeros((experts, toks), F32)
    for k in range(ids.shape[0]):
        hit = e_iota == ids[k : k + 1, :]
        named = named | hit
        weight = weight + jnp.where(hit, gates[k : k + 1, :], 0.0)
    earlier = lax.broadcasted_iota(jnp.int32, (toks, toks), 0) < lax.broadcasted_iota(jnp.int32, (toks, toks), 1)
    slot = jnp.dot(
        jnp.where(named, 1.0, 0.0).astype(BF), jnp.where(earlier, 1.0, 0.0).astype(BF), preferred_element_type=F32)
    slot = jnp.where(named, slot, -1.0)
    slots[first_at] = slot

    with jax.named_scope("norm"):
        values = tok[...].astype(F32)
        average = jnp.mean(values, axis=-1, keepdims=True)
        centered = values - average
        variance = jnp.mean(centered * centered, axis=-1, keepdims=True)
        normed = (centered * lax.rsqrt(variance + 1e-05) * gain[...]).astype(BF)
        for cc in range(2):
            @pl.when(c == cc)
            def _():
                for f in range(PIECES):
                    line[f, first_at] = normed[:, half * cc + fine * f : half * cc + fine * (f + 1)]

    def remote(src, dst, send_sem, recv_sem, to):
        return pltpu.make_async_remote_copy(
            src_ref=src, dst_ref=dst, send_sem=send_sem, recv_sem=recv_sem, device_id=to, device_id_type=MESH)

    with jax.named_scope("entry_wait"):
        pl.semaphore_wait(barrier, 2 * len(XY) + NZ)
    mates = [(sec, on_first(lax.rem(first_at + k, SIDE))) for k in (1, 3, 2)]
    for to in mates:
        remote(slots.at[first_at], slots.at[first_at], ns.at[0], nr.at[0], to).start()
    for f in range(PIECES):
        for to in mates:
            remote(line.at[f, first_at], line.at[f, first_at], ls.at[0], lr.at[f], to).start()

    def shares(low, count, hi, lo):
        places = lax.broadcasted_iota(jnp.int32, (count, toks), 0).astype(F32) + float(low)
        rows = [jnp.where(slot[e : e + 1, :] == places, weight[e : e + 1, :], 0.0) for e in range(experts)]
        share = jnp.transpose(jnp.concatenate(rows, axis=0))
        top = share.astype(BF)
        hi[...] = top
        lo[...] = (share - top.astype(F32)).astype(BF)

    with jax.named_scope("shares"):
        for j in range(ALONE):
            shares(SLOTS * j, SLOTS, chi.at[j], clo.at[j])
        shares(SLOTS * ALONE, SLOTS * late, chi2, clo2)

    def block_rows(i):
        return pl.ds(pl.multiple_of(SLOTS * on_first(i), SLOTS), SLOTS)

    s_iota = lax.broadcasted_iota(jnp.int32, (SLOTS, toks), 0).astype(F32)

    def picks(js, i):
        rows = []
        for j in js:
            for q in range(SIDE):
                row = slots[i, pl.ds(on_then(q), 1), :]
                rows.append(jnp.where((row - float(SLOTS * j)) == s_iota, 1.0, 0.0).astype(BF))
        return jnp.concatenate(rows, axis=0)

    @jax.named_scope("pack")
    def pack(js, f):
        cols = slice(fine * f, fine * (f + 1))
        for i in range(SIDE):
            rows = jnp.dot(picks(js, i), line[f, i], preferred_element_type=F32).astype(BF)
            for n, j in enumerate(js):
                for q in range(SIDE):
                    at = SLOTS * (n * SIDE + q)
                    packed[j, q, i, :, cols] = rows[at : at + SLOTS, :]
        for j in js:
            for i in range(SIDE):
                xin[j, 0, block_rows(i), cols] = packed[j, then_at, i, :, cols]

    def dispatch(j, cols):
        for k in (1, 3, 2):
            q = lax.rem(then_at + k, SIDE)
            for i in range(SIDE):
                remote(
                    packed.at[j, q, i, :, cols], xin.at[j, 0, block_rows(i), cols], xs.at[0], xr.at[j],
                    (sec, on_then(q))).start()

    await_bytes(slots.at[pl.ds(0, SIDE - 1)], nr.at[0])
    for f in range(PIECES):
        with jax.named_scope("line_wait"):
            await_bytes(line.at[f, pl.ds(0, SIDE - 1)], lr.at[f])
        pack([0], f)
        dispatch(0, pl.ds(fine * f, fine))
    for f in range(PIECES):
        pack(list(range(1, BATCHES)), f)
    every = pl.ds(0, half)
    dispatch(1, every)

    def sib_x(j):
        return remote(xin.at[j, 0], xin.at[j, 1], fs.at[0], fr.at[j], sibling)

    own_rows = pl.ds(pl.multiple_of(hrows * c, hrows), hrows)
    sib_rows = pl.ds(pl.multiple_of(hrows * (1 - c), hrows), hrows)

    def sib_p(j, g):
        return remote(part.at[j, g, sib_rows, :], sib.at[j, g], ps.at[0], pr.at[j, g], sibling)

    def own_sum(j, k, first, count):
        g, i = PLACE[k % NZ]
        cols = slice(chunk * i + first, chunk * i + first + count)
        return part[j, g, own_rows, cols].astype(F32) + sib[j, g, :, cols].astype(F32)

    def sign(j):
        return 1 - 2 * (j % 2)

    def chain_a(j, t):
        return remote(asend.at[j, t], arecv.at[j, t], as_.at[0], ar.at[j, t], zdev(-sign(j)))

    def chain_b(j, t):
        return remote(bsend.at[j, t], brecv.at[j, t], bs.at[0], br.at[j, t], zdev(sign(j)))

    @jax.named_scope("chain_step")
    def chain_step(j, t):
        if j < 0 or j >= ALONE:
            return
        ka, kb = 4 + sign(j) * t, 4 - sign(j) * (1 + t)
        if t < 2:
            sib_p(j, t).wait_recv()
        total = own_sum(j, ka, 0, chunk)
        if t > 0:
            chain_a(j, t - 1).wait_recv()
            total = total + arecv[j, t - 1].astype(F32)
        asend[j, t] = total.astype(BF)
        chain_a(j, t).start()
        if t < 3:
            total = own_sum(j, kb, 0, chunk)
            if t > 0:
                chain_b(j, t - 1).wait_recv()
                total = total + brecv[j, t - 1].astype(F32)
            bsend[j, t] = total.astype(BF)
            chain_b(j, t).start()

    def late_a(p, t):
        return remote(asend2.at[p, t], arecv2.at[p, t], as2.at[0], ar2.at[p, t], zdev(-sign(p)))

    def late_b(p, t):
        return remote(bsend2.at[p, t], brecv2.at[p, t], bs2.at[0], br2.at[p, t], zdev(sign(p)))

    @jax.named_scope("late_step")
    def late_step(p, t):
        ka, kb = 4 + sign(p) * t, 4 - sign(p) * (1 + t)
        if p == 0 and t < 2:
            for j in range(ALONE, BATCHES):
                sib_p(j, t).wait_recv()
        for k, send, recv, step in ((ka, asend2, arecv2, late_a), (kb, bsend2, brecv2, late_b)):
            if send is bsend2 and t == 3:
                continue
            if t > 0:
                step(p, t - 1).wait_recv()
            for n in range(late):
                lines = slice(hrows * n, hrows * (n + 1))
                total = own_sum(ALONE + n, k, col * p, col)
                if t > 0:
                    total = total + recv[p, t - 1, lines, :].astype(F32)
                send[p, t, lines, :] = total.astype(BF)
            step(p, t).start()

    def give_back(src, dst, height, send_sem, recv_sem):
        mine = pl.ds(pl.multiple_of(height * me, height), height)
        for i in range(blocks):
            b = c * blocks + i
            rows = pl.ds(height * i, height)

            @pl.when(b != me)
            def _():
                remote(src.at[rows, :], dst.at[mine, :], send_sem, recv_sem, (sec, b)).start()

            @pl.when(b == me)
            def _():
                dst[mine, :] = src[rows, :]

            remote(src.at[rows, :], dst.at[mine, :], send_sem, recv_sem, (other, b)).start()

    home = c == me // blocks

    def await_rows(ref, height, sem):
        @pl.when(home)
        def _():
            await_bytes(ref.at[pl.ds(0, height * (experts - 1)), :], sem)

        @pl.when(jnp.logical_not(home))
        def _():
            await_bytes(ref, sem)

    @jax.named_scope("chain_end")
    def chain_end(j):
        chain_a(j, 3).wait_recv()
        chain_b(j, 2).wait_recv()
        total = own_sum(j, 0, 0, chunk) + arecv[j, 3].astype(F32) + brecv[j, 2].astype(F32)
        ret_out[j] = total.astype(BF)
        give_back(ret_out.at[j], ret.at[j], SLOTS, rs.at[j], rr.at[j])

    @jax.named_scope("late_end")
    def late_end(p):
        late_a(p, 3).wait_recv()
        late_b(p, 2).wait_recv()
        for n in range(late):
            lines = slice(hrows * n, hrows * (n + 1))
            total = own_sum(ALONE + n, 0, col * p, col)
            total = total + arecv2[p, 3, lines, :].astype(F32) + brecv2[p, 2, lines, :].astype(F32)
            total = total.astype(BF)
            for i in range(blocks):
                at = SLOTS * (late * i + n)
                ret_out2[p, at : at + SLOTS, :] = total[SLOTS * i : SLOTS * (i + 1), :]
        give_back(ret_out2.at[p], ret2.at[p], SLOTS * late, rs.at[ALONE + p], rr2.at[p])

    own_toks = pl.ds(pl.multiple_of(htoks * c, htoks), htoks)

    @jax.named_scope("mix")
    def mix(j):
        await_rows(ret.at[j], SLOTS, rr.at[j])
        term = jnp.dot(chi[j], ret[j], preferred_element_type=F32)
        term = term + jnp.dot(clo[j], ret[j], preferred_element_type=F32)
        acc[...] = term if j == 0 else acc[...] + term

    def give(p, k):
        here = mixed.at[p, z, own_toks, :]
        return remote(here, here, os_.at[0], or_.at[p], zdev(k))

    def hand(p):
        here = mixed.at[p, :, own_toks, :]
        return remote(here, here, gs.at[0], gr.at[p], sibling)

    @jax.named_scope("late_mix")
    def late_mix(p):
        await_rows(ret2.at[p], SLOTS * late, rr2.at[p])
        term = jnp.dot(chi2[...], ret2[p], preferred_element_type=F32)
        term = term + jnp.dot(clo2[...], ret2[p], preferred_element_type=F32)
        cols = slice(col * p, col * (p + 1))
        acc[:, cols] = acc[:, cols] + term
        mixed[p, z, own_toks, :] = acc[own_toks, cols].astype(BF)
        for k in (4, 3, 5, 2, 6, 1, 7):
            give(p, k).start()

    @jax.named_scope("take")
    def take(j):
        if j >= BATCHES:
            return
        await_bytes(xin.at[j, 0, pl.ds(0, SLOTS * SIDE * (SIDE - 1)), :], xr.at[j])
        if j + 2 < BATCHES:
            dispatch(j + 2, every)
        sib_x(j).start()

    @jax.named_scope("up")
    def up(j, h):
        gate = jnp.dot(xin[j, h], wg[h], preferred_element_type=F32)
        raised = jnp.dot(xin[j, h], wu[h], preferred_element_type=F32)
        if h == 0:
            gacc[...] = gate
            uacc[...] = raised
            return None
        gate = gacc[...] + gate
        raised = uacc[...] + raised
        return (gate / (1.0 + jnp.exp(-gate)) * raised).astype(BF)

    @jax.named_scope("down")
    def down(j, hidden):
        for g in range(2):
            part[j, g] = jnp.dot(hidden, wd[g], preferred_element_type=F32).astype(BF)
            sib_p(j, g).start()

    take(0)
    for j in range(BATCHES):
        if j == 0:
            loads[0].wait()
            loads[1].wait()
        up(j, 0)
        if j == 0:
            loads[2].wait()
            loads[3].wait()
        with jax.named_scope("sib_wait"):
            sib_x(j).wait_recv()
        hidden = up(j, 1)
        if j == 0:
            await_bytes(wd, w_sem.at[4])
        down(j, hidden)
        take(j + 1)
        for t in range(1, 4):
            chain_step(j - t, t)
        chain_step(j, 0)
    for p in range(PIECES):
        late_step(p, 0)
    for p in range(PIECES):
        late_step(p, 1)
    chain_step(1, 3)
    chain_end(0)
    for p in range(PIECES):
        late_step(p, 2)
    chain_end(1)
    mix(0)
    for p in range(PIECES):
        late_step(p, 3)
    mix(1)
    for p in range(PIECES):
        late_end(p)
    for p in range(PIECES):
        late_mix(p)

    with jax.named_scope("drain"):
        await_bytes(slots.at[pl.ds(0, SIDE - 1)], ns.at[0])
        await_bytes(line.at[:, pl.ds(0, SIDE - 1)], ls.at[0])
        await_bytes(packed.at[:, pl.ds(0, SIDE - 1)], xs.at[0])
        await_bytes(xin.at[:, 0], fs.at[0])
        await_bytes(part.at[:, :, pl.ds(0, hrows), :], ps.at[0])
        await_bytes(asend, as_.at[0])
        await_bytes(bsend, bs.at[0])
        await_bytes(asend2, as2.at[0])
        await_bytes(bsend2, bs2.at[0])
        for j in range(ALONE):
            await_rows(ret.at[j], SLOTS, rs.at[j])
        for p in range(PIECES):
            await_rows(ret2.at[p], SLOTS * late, rs.at[ALONE + p])
    for p in range(PIECES):
        with jax.named_scope("gather_wait"):
            await_bytes(mixed.at[p, pl.ds(0, NZ - 1), pl.ds(0, htoks), :], or_.at[p])
        hand(p).start()
    for p in range(PIECES):
        with jax.named_scope("hand_wait"):
            hand(p).wait_recv()
        for k in range(NZ):
            out[:, chunk * k + col * p : chunk * k + col * (p + 1)] = mixed[p, k]
    await_bytes(mixed.at[:, pl.ds(0, NZ - 1), pl.ds(0, htoks), :], os_.at[0])
    await_bytes(mixed.at[:, :, pl.ds(0, htoks), :], gs.at[0])


def on_device(tokens, norm_gain, expert_ids, gates, gate_proj, up_proj, down_proj):
    toks, features = tokens.shape
    experts = lax.axis_size("expert")
    width = gate_proj.shape[2]
    half, chunk = features // 2, features // NZ
    fine, col = half // PIECES, chunk // PIECES
    rows = experts * SLOTS
    hrows = rows // 2
    late = BATCHES - ALONE
    dma = pltpu.SemaphoreType.DMA
    vmem = pl.BlockSpec(memory_space=pltpu.VMEM)
    hbm = pl.BlockSpec(memory_space=pl.ANY)
    b = BATCHES
    scratch = [
        pltpu.VMEM((2, half, width), BF),
        pltpu.VMEM((2, half, width), BF),
        pltpu.VMEM((2, width, half), BF),
        pltpu.VMEM((PIECES, SIDE, toks, fine), BF),
        pltpu.VMEM((SIDE, experts, toks), F32),
        pltpu.VMEM((ALONE, toks, rows), BF),
        pltpu.VMEM((ALONE, toks, rows), BF),
        pltpu.VMEM((toks, rows * late), BF),
        pltpu.VMEM((toks, rows * late), BF),
        pltpu.VMEM((b, SIDE, SIDE, SLOTS, half), BF),
        pltpu.VMEM((b, 2, rows, half), BF),
        pltpu.VMEM((rows, width), F32),
        pltpu.VMEM((rows, width), F32),
        pltpu.VMEM((b, 2, rows, half), BF),
        pltpu.VMEM((b, 2, hrows, half), BF),
        pltpu.VMEM((ALONE, 4, hrows, chunk), BF),
        pltpu.VMEM((ALONE, 4, hrows, chunk), BF),
        pltpu.VMEM((ALONE, 3, hrows, chunk), BF),
        pltpu.VMEM((ALONE, 3, hrows, chunk), BF),
        pltpu.VMEM((PIECES, 4, hrows * late, col), BF),
        pltpu.VMEM((PIECES, 4, hrows * late, col), BF),
        pltpu.VMEM((PIECES, 3, hrows * late, col), BF),
        pltpu.VMEM((PIECES, 3, hrows * late, col), BF),
        pltpu.VMEM((ALONE, hrows, chunk), BF),
        pltpu.VMEM((ALONE, rows, chunk), BF),
        pltpu.VMEM((PIECES, hrows * late, col), BF),
        pltpu.VMEM((PIECES, rows * late, col), BF),
        pltpu.VMEM((toks, chunk), F32),
        pltpu.VMEM((PIECES, NZ, toks, col), BF),
        dma((5,)),
        dma((1,)), dma((PIECES,)),
        dma((1,)), dma((1,)),
        dma((1,)), dma((b,)),
        dma((1,)), dma((b,)),
        dma((1,)), dma((b, 2)),
        dma((1,)), dma((ALONE, 4)),
        dma((1,)), dma((ALONE, 3)),
        dma((1,)), dma((PIECES, 4)),
        dma((1,)), dma((PIECES, 3)),
        dma((ALONE + PIECES,)), dma((ALONE,)), dma((PIECES,)),
        dma((1,)), dma((PIECES,)),
        dma((1,)), dma((PIECES,)),
    ]
    return pl.pallas_call(
        kernel,
        out_shape=pltpu.VMEM((toks, features), BF),
        in_specs=[vmem, vmem, vmem, vmem, hbm, hbm, hbm],
        out_specs=vmem,
        scratch_shapes=scratch,
        compiler_params=pltpu.CompilerParams(
            collective_id=0, has_side_effects=True, vmem_limit_bytes=60 << 20
        ),
    )(tokens, norm_gain.reshape(1, -1), expert_ids.T, gates.T, gate_proj, up_proj, down_proj)


def solution(mesh):
    return jax.shard_map(
        on_device,
        mesh=mesh,
        in_specs=(
            P("expert", None),
            P(),
            P("expert", None),
            P("expert", None),
            P("expert", None, "section"),
            P("expert", None, "section"),
            P("expert", "section", None),
        ),
        out_specs=P("expert", None),
        check_vma=False,
    )
```

time: 263 us -> 95.2 us (0.36)
  waiting for transfers between devices: 110 us -> 0 us
  Pallas kernels: 0 us -> 94.2 us
  blocking collectives: 93.9 us -> 0 us
  matrix products: 26.6 us -> 0 us
  between operations: 13.5 us -> 0.01 us
  local copies, waits for them, and re-layouts: 12.9 us -> 0.88 us
  other arithmetic: 5.59 us -> 0 us
    pallas_call x0 -> x1, Pallas kernels: none -> 94.2 us  [on_device(): pl.pallas_call(kernel, out_shape=pltpu.VMEM((toks, features), BF), in_spe...]
    all_to_all x2 -> x0, blocking collectives: 93.9 us -> none  [the longest x1 79.6 us: on_device(): lax.all_to_all(packed, 'expert', split_axis=0, concat_axis=0, tiled=True)]
    reduce_scatter x1 -> x0, waiting for transfers between devices: 65.6 us -> none  [on_device(): lax.psum_scatter(jnp.dot(part_rows, down_weight, preferred_element_type=j...]
    all_gather x1 -> x0, waiting for transfers between devices: 44.4 us -> none  [on_device(): all_slots = lax.all_gather(returned, 'section', axis=0, tiled=True)]
    dot_general x6 -> x0, matrix products: 26.6 us -> none  [the longest x1 6.5 us: on_device(): jnp.dot(combine, all_slots.reshape(-1, features).astype(jnp.float32), pre...]
    reshape x3 -> x0, local copies, waits for them, and re-layouts: 7.77 us -> none  [the longest x1 5.89 us: on_device(): spread = jnp.repeat(normed, top_count, axis=0)]
    reduce_sum x3 -> x0, other arithmetic: 2.91 us -> none  [the longest x1 1.49 us: on_device(): variance = jnp.mean(centered * centered, axis=-1, keepdims=True)]
  transfers between devices with their start and end apart: 2 -> 0, of which waited for: 2 -> 0; matrix products, arithmetic and copies ran while one was open for 1% -> 0% of each run, Pallas kernels for 0% -> 0%
where the time goes in v2:
time: 95.2 us; the launch traced here: 95.1 us
  Pallas kernels  94.2 us (99%)
    pallas_call x1, Pallas kernels, on_device(): pl.pallas_call(kernel, out_shape=pltpu.VMEM((toks, features), BF), in_spe...  94.2 us

profile of v2, /device:TPU:1, one launch (start us, length us, event | category | flops | bytes accessed | tf_op | source)
XLA Modules:
  0.0 95.1 jit_solution(4672280880554015681)
XLA Ops:
  0.0 94.2 %shard_map.73 = bf16[128,3072]{1,0:T(8,128)(2,1)S(1)} custom-call(bf16[128,3072]{1,0:T(8,128)(2,1)} %tok.1, f32[1,3072]{1,0:T(1,128)} %bitcast.3, s32[4,128]{1,0:T(4,128)} %bitcast.4, f32[4,128]{1,0:T(4,128)} %bitcast.5, bf16[1,3072,512]{2,1,0:T(8,128)(2,1)} %wg_hbm.1, bf16[1,3072,512]{2,1,0:T(8,128)(2,1)} %wu_hbm.1, bf16[1,512,3072]{2,1,0:T(8,128)(2,1)} %wd_hbm.1), custom_call_target="tpu_custom_call" | custom-call | tf_op jit(solution)/shard_map/pallas_call | solution.py:472
  94.3 0.9 copy.9

commit v3 on v2

v3 whole, which is shorter than its diff:
```python
import jax
import jax.numpy as jnp
from jax import lax
from jax.experimental import pallas as pl
from jax.experimental.pallas import tpu as pltpu
from jax.sharding import PartitionSpec as P

MESH = pl.DeviceIdType.MESH
BATCHES = 4
CHAINS = 2
SLOTS = 16
NZ = 8
SIDE = 4
XY = [(dx, dy) for dx in range(SIDE) for dy in range(SIDE) if (dx, dy) != (0, 0)]
ORDER = ((4, 3, 5, 2), (6, 1, 7, 0))
PLACE = {k: (g, i) for g, ks in enumerate(ORDER) for i, k in enumerate(ks)}
PIECES = 3
PARTS = 2
BF = jnp.bfloat16
F32 = jnp.float32


def kernel(
    tok, gain, ids, gates, wg_hbm, wu_hbm, wd_hbm, out,
    wg, wu, wd, line, slots, chi, clo, packed, xin, gacc, uacc, part, sib,
    asend, arecv, bsend, brecv, ret_out, ret, late_out, late_in, zsend, zrecv, acc, mixed,
    w_sem, ls, lr, ns, nr, xs, xr, fs, fr, ps, pr, as_, ar, bs, br, rs, rr, rl, zs, zr, os_, or_, gs, gr,
):
    sec, me = lax.axis_index("section"), lax.axis_index("expert")
    z, c = sec // 2, sec % 2
    x, y = me // SIDE, me % SIDE
    experts = SIDE * SIDE
    blocks = experts // 2
    toks = tok.shape[0]
    htoks = toks // 2
    fine = line.shape[4]
    wide = fine * PARTS
    half = 2 * wide
    col = mixed.shape[3]
    chunk = col * PIECES
    hrows = blocks * SLOTS
    first_at, then_at = (x, y), (y, x)

    def on_first(f, i):
        return i * SIDE + y if f == 0 else x * SIDE + i

    def on_then(f, q):
        return x * SIDE + q if f == 0 else q * SIDE + y

    def zdev(dz, core=c):
        return (lax.rem(z + dz + 2 * NZ, NZ) * 2 + core, me)

    def xydev(dx, dy):
        return lax.rem(x + dx, SIDE) * SIDE + lax.rem(y + dy, SIDE)

    other = z * 2 + 1 - c
    sibling = (other, me)

    barrier = pltpu.get_barrier_semaphore()
    for dx, dy in XY:
        for s in (sec, other):
            pl.semaphore_signal(barrier, inc=1, device_id=(s, xydev(dx, dy)), device_id_type=MESH)
    pl.semaphore_signal(barrier, inc=1, device_id=sibling, device_id_type=MESH)
    for k in range(1, NZ):
        for core in range(2):
            pl.semaphore_signal(barrier, inc=1, device_id=zdev(k, core), device_id_type=MESH)

    loads = []
    for h in range(2):
        lines = pl.ds(pl.multiple_of(half * lax.rem(c + h, 2), half), half)
        loads.append(pltpu.make_async_copy(wg_hbm.at[0, lines, :], wg.at[h], w_sem.at[2 * h]))
        loads.append(pltpu.make_async_copy(wu_hbm.at[0, lines, :], wu.at[h], w_sem.at[2 * h + 1]))
    for load in loads:
        load.start()
    for k in range(NZ):
        cols = pl.ds(pl.multiple_of(chunk * lax.rem(z + k, NZ), chunk), chunk)
        g, i = PLACE[k]
        pltpu.make_async_copy(wd_hbm.at[0, :, cols], wd.at[g, :, pl.ds(chunk * i, chunk)], w_sem.at[4]).start()

    def await_bytes(ref, sem):
        pltpu.make_async_copy(ref, ref, sem).wait()

    e_iota = lax.broadcasted_iota(jnp.int32, (experts, toks), 0)
    named = jnp.zeros((experts, toks), jnp.bool_)
    weight = jnp.zeros((experts, toks), F32)
    for k in range(ids.shape[0]):
        hit = e_iota == ids[k : k + 1, :]
        named = named | hit
        weight = weight + jnp.where(hit, gates[k : k + 1, :], 0.0)
    earlier = lax.broadcasted_iota(jnp.int32, (toks, toks), 0) < lax.broadcasted_iota(jnp.int32, (toks, toks), 1)
    slot = jnp.dot(
        jnp.where(named, 1.0, 0.0).astype(BF), jnp.where(earlier, 1.0, 0.0).astype(BF), preferred_element_type=F32)
    slot = jnp.where(named, slot, -1.0)
    for f in range(2):
        slots[f, first_at[f]] = slot

    with jax.named_scope("norm"):
        values = tok[...].astype(F32)
        average = jnp.mean(values, axis=-1, keepdims=True)
        centered = values - average
        variance = jnp.mean(centered * centered, axis=-1, keepdims=True)
        normed = (centered * lax.rsqrt(variance + 1e-05) * gain[...]).astype(BF)
        for cc in range(2):
            @pl.when(c == cc)
            def _():
                for f in range(2):
                    for s in range(PARTS):
                        at = half * cc + wide * f + fine * s
                        line[f, s, first_at[f]] = normed[:, at : at + fine]

    def remote(src, dst, send_sem, recv_sem, to):
        return pltpu.make_async_remote_copy(
            src_ref=src, dst_ref=dst, send_sem=send_sem, recv_sem=recv_sem, device_id=to, device_id_type=MESH)

    with jax.named_scope("entry_wait"):
        pl.semaphore_wait(barrier, 2 * len(XY) + 2 * NZ - 1)
    def mates(f):
        return [(sec, on_first(f, lax.rem(first_at[f] + k, SIDE))) for k in (1, 3, 2)]

    for f in range(2):
        for to in mates(f):
            here = slots.at[f, first_at[f]]
            remote(here, here, ns.at[0], nr.at[f], to).start()
    for s in range(PARTS):
        for f in range(2):
            for to in mates(f):
                here = line.at[f, s, first_at[f]]
                remote(here, here, ls.at[0], lr.at[f, s], to).start()

    def shares(low, count, hi, lo):
        places = lax.broadcasted_iota(jnp.int32, (count, toks), 0).astype(F32) + float(low)
        rows = [jnp.where(slot[e : e + 1, :] == places, weight[e : e + 1, :], 0.0) for e in range(experts)]
        share = jnp.transpose(jnp.concatenate(rows, axis=0))
        top = share.astype(BF)
        hi[...] = top
        lo[...] = (share - top.astype(F32)).astype(BF)

    with jax.named_scope("shares"):
        for j in range(BATCHES):
            shares(SLOTS * j, SLOTS, chi.at[j], clo.at[j])

    def block_rows(f, i):
        return pl.ds(pl.multiple_of(SLOTS * on_first(f, i), SLOTS), SLOTS)

    s_iota = lax.broadcasted_iota(jnp.int32, (SLOTS, toks), 0).astype(F32)

    def picks(js, f, i):
        rows = []
        for j in js:
            for q in range(SIDE):
                row = slots[f, i, pl.ds(on_then(f, q), 1), :]
                rows.append(jnp.where((row - float(SLOTS * j)) == s_iota, 1.0, 0.0).astype(BF))
        return jnp.concatenate(rows, axis=0)

    @jax.named_scope("pack")
    def pack(js, f, parts):
        for i in range(SIDE):
            chosen = picks(js, f, i)
            for s in parts:
                cols = slice(fine * s, fine * (s + 1))
                rows = jnp.dot(chosen, line[f, s, i], preferred_element_type=F32).astype(BF)
                for n, j in enumerate(js):
                    for q in range(SIDE):
                        at = SLOTS * (n * SIDE + q)
                        packed[j, f, q, i, :, cols] = rows[at : at + SLOTS, :]
        for j in js:
            for i in range(SIDE):
                for s in parts:
                    cols = slice(fine * s, fine * (s + 1))
                    to = slice(wide * f + fine * s, wide * f + fine * (s + 1))
                    xin[j, 0, block_rows(f, i), to] = packed[j, f, then_at[f], i, :, cols]

    def dispatch(j, f, first, count):
        for k in (1, 3, 2):
            q = lax.rem(then_at[f] + k, SIDE)
            for i in range(SIDE):
                remote(
                    packed.at[j, f, q, i, :, pl.ds(first, count)],
                    xin.at[j, 0, block_rows(f, i), pl.ds(wide * f + first, count)], xs.at[0], xr.at[j],
                    (sec, on_then(f, q))).start()

    for f in range(2):
        await_bytes(slots.at[f, pl.ds(0, SIDE - 1)], nr.at[f])
    for s in range(PARTS):
        for f in range(2):
            with jax.named_scope("line_wait"):
                await_bytes(line.at[f, s, pl.ds(0, SIDE - 1)], lr.at[f, s])
            pack([0], f, [s])
            dispatch(0, f, fine * s, fine)

    def dispatch_all(j):
        for f in range(2):
            dispatch(j, f, 0, wide)

    for f in range(2):
        pack(list(range(1, BATCHES)), f, range(PARTS))
    dispatch_all(1)

    def sib_x(j):
        return remote(xin.at[j, 0], xin.at[j, 1], fs.at[0], fr.at[j], sibling)

    own_rows = pl.ds(pl.multiple_of(hrows * c, hrows), hrows)
    sib_rows = pl.ds(pl.multiple_of(hrows * (1 - c), hrows), hrows)

    def sib_p(j, g):
        return remote(part.at[j, g, sib_rows, :], sib.at[j, g], ps.at[0], pr.at[j, g], sibling)

    def own_sum(j, k, first, count):
        g, i = PLACE[k % NZ]
        cols = slice(chunk * i + first, chunk * i + first + count)
        return part[j, g, own_rows, cols].astype(F32) + sib[j, g, :, cols].astype(F32)

    def sign(j):
        return 1 - 2 * (j % 2)

    def chain_a(j, t):
        return remote(asend.at[j, t], arecv.at[j, t], as_.at[0], ar.at[j, t], zdev(-sign(j)))

    def chain_b(j, t):
        return remote(bsend.at[j, t], brecv.at[j, t], bs.at[0], br.at[j, t], zdev(sign(j)))

    @jax.named_scope("chain_step")
    def chain_step(j, t):
        if j < 0 or j >= CHAINS:
            return
        ka, kb = 4 + sign(j) * t, 4 - sign(j) * (1 + t)
        if t < 2:
            sib_p(j, t).wait_recv()
        total = own_sum(j, ka, 0, chunk)
        if t > 0:
            chain_a(j, t - 1).wait_recv()
            total = total + arecv[j, t - 1].astype(F32)
        asend[j, t] = total.astype(BF)
        chain_a(j, t).start()
        if t < 3:
            total = own_sum(j, kb, 0, chunk)
            if t > 0:
                chain_b(j, t - 1).wait_recv()
                total = total + brecv[j, t - 1].astype(F32)
            bsend[j, t] = total.astype(BF)
            chain_b(j, t).start()

    mine = pl.ds(pl.multiple_of(SLOTS * me, SLOTS), SLOTS)

    def give_back(srcs, dst, send_sem, recv_sem):
        for core, src in enumerate(srcs):
            for i in range(blocks):
                b = c * blocks + i
                rows = pl.ds(SLOTS * i, SLOTS)
                own = jnp.logical_and(b == me, c == core)

                @pl.when(jnp.logical_not(own))
                def _():
                    remote(src.at[rows, :], dst.at[mine, :], send_sem, recv_sem, (z * 2 + core, b)).start()

                @pl.when(own)
                def _():
                    dst[mine, :] = src[rows, :]

    home = c == me // blocks

    def await_rows(ref, sem):
        @pl.when(home)
        def _():
            await_bytes(ref.at[pl.ds(0, SLOTS * (experts - 1)), :], sem)

        @pl.when(jnp.logical_not(home))
        def _():
            await_bytes(ref, sem)

    @jax.named_scope("chain_end")
    def chain_end(j):
        chain_a(j, 3).wait_recv()
        chain_b(j, 2).wait_recv()
        total = own_sum(j, 0, 0, chunk) + arecv[j, 3].astype(F32) + brecv[j, 2].astype(F32)
        ret_out[j] = total.astype(BF)
        give_back([ret_out.at[j]] * 2, ret.at[j], rs.at[j], rr.at[j])

    @jax.named_scope("late_back")
    def late_back(j):
        n = j - CHAINS
        for g in range(2):
            sib_p(j, g).wait_recv()
            total = (part[j, g, own_rows, :].astype(F32) + sib[j, g].astype(F32)).astype(BF)
            for i in range(NZ // 2):
                late_out[n, i, g] = total[:, chunk * i : chunk * (i + 1)]
        for i in range(NZ // 2):
            give_back([late_out.at[n, i, 0], late_out.at[n, i, 1]], late_in.at[n, i], rs.at[j], rl.at[n, i])

    own_toks = pl.ds(pl.multiple_of(htoks * c, htoks), htoks)

    @jax.named_scope("mix")
    def mix(j):
        await_rows(ret.at[j], rr.at[j])
        term = jnp.dot(chi[j], ret[j], preferred_element_type=F32)
        term = term + jnp.dot(clo[j], ret[j], preferred_element_type=F32)
        acc[...] = term if j == 0 else acc[...] + term

    def give(p, k):
        here = mixed.at[p, z, own_toks, :]
        return remote(here, here, os_.at[0], or_.at[p], zdev(k))

    def hand(p):
        here = mixed.at[p, :, own_toks, :]
        return remote(here, here, gs.at[0], gr.at[p], sibling)

    @jax.named_scope("late_mix")
    def late_mix(i):
        term = jnp.zeros((toks, chunk), F32)
        for n in range(BATCHES - CHAINS):
            await_rows(late_in.at[n, i], rl.at[n, i])
            term = term + jnp.dot(chi[CHAINS + n], late_in[n, i], preferred_element_type=F32)
            term = term + jnp.dot(clo[CHAINS + n], late_in[n, i], preferred_element_type=F32)
        zsend[i] = term.astype(BF)
        k = ORDER[0][i] * (1 - c) + ORDER[1][i] * c
        for core in range(2):
            copy = remote(
                zsend.at[i, pl.ds(htoks * core, htoks), :], zrecv.at[k], zs.at[0], zr.at[0], zdev(k, core))
            if ORDER[1][i] == 0 and core == 1:
                @pl.when(c == 0)
                def _():
                    copy.start()

                @pl.when(c == 1)
                def _():
                    zrecv[0] = zsend[i, htoks:, :]
            else:
                copy.start()

    def await_parts(ref, sem):
        @pl.when(c == 0)
        def _():
            await_bytes(ref, sem)

        @pl.when(c == 1)
        def _():
            await_bytes(ref.at[pl.ds(0, NZ - 1)], sem)

    @jax.named_scope("gather")
    def gather():
        await_parts(zrecv, zr.at[0])
        for p in range(PIECES):
            cols = slice(col * p, col * (p + 1))
            total = acc[own_toks, cols]
            for k in range(NZ):
                total = total + zrecv[k, :, cols].astype(F32)
            mixed[p, z, own_toks, :] = total.astype(BF)
            for k in (4, 3, 5, 2, 6, 1, 7):
                give(p, k).start()

    @jax.named_scope("take")
    def take(j):
        if j >= BATCHES:
            return
        await_bytes(xin.at[j, 0, pl.ds(0, SLOTS * SIDE * (SIDE - 1)), :], xr.at[j])
        if j + 2 < BATCHES:
            dispatch_all(j + 2)
        sib_x(j).start()

    @jax.named_scope("up")
    def up(j, h):
        gate = jnp.dot(xin[j, h], wg[h], preferred_element_type=F32)
        raised = jnp.dot(xin[j, h], wu[h], preferred_element_type=F32)
        if h == 0:
            gacc[...] = gate
            uacc[...] = raised
            return None
        gate = gacc[...] + gate
        raised = uacc[...] + raised
        return (gate / (1.0 + jnp.exp(-gate)) * raised).astype(BF)

    @jax.named_scope("down")
    def down(j, hidden):
        for g in range(2):
            part[j, g] = jnp.dot(hidden, wd[g], preferred_element_type=F32).astype(BF)
            sib_p(j, g).start()

    def after(j):
        if j < 0:
            return
        if j >= CHAINS:
            late_back(j)
        for t in range(4):
            chain_step(j - t, t)

    take(0)
    for j in range(BATCHES):
        if j == 0:
            loads[0].wait()
            loads[1].wait()
        up(j, 0)
        after(j - 1)
        if j == 0:
            loads[2].wait()
            loads[3].wait()
        with jax.named_scope("sib_wait"):
            sib_x(j).wait_recv()
        hidden = up(j, 1)
        if j == 0:
            await_bytes(wd, w_sem.at[4])
        take(j + 1)
        down(j, hidden)
    after(BATCHES - 1)
    chain_step(1, 3)
    chain_end(0)
    late_mix(0)
    chain_end(1)
    late_mix(1)
    late_mix(2)
    late_mix(3)
    mix(0)
    mix(1)
    gather()

    with jax.named_scope("drain"):
        await_bytes(slots.at[:, pl.ds(0, SIDE - 1)], ns.at[0])
        await_bytes(line.at[:, :, pl.ds(0, SIDE - 1)], ls.at[0])
        await_bytes(packed.at[:, :, pl.ds(0, SIDE - 1)], xs.at[0])
        await_bytes(xin.at[:, 0], fs.at[0])
        await_bytes(part.at[:, :, pl.ds(0, hrows), :], ps.at[0])
        await_bytes(asend, as_.at[0])
        await_bytes(bsend, bs.at[0])
        for j in range(CHAINS):
            await_rows(ret.at[j], rs.at[j])
        for n in range(BATCHES - CHAINS):
            for i in range(NZ // 2):
                await_rows(late_in.at[n, i], rs.at[CHAINS + n])
        await_parts(zrecv, zs.at[0])

    for p in range(PIECES):
        with jax.named_scope("gather_wait"):
            await_bytes(mixed.at[p, pl.ds(0, NZ - 1), pl.ds(0, htoks), :], or_.at[p])
        hand(p).start()
    for p in range(PIECES):
        with jax.named_scope("hand_wait"):
            hand(p).wait_recv()
        for k in range(NZ):
            out[:, chunk * k + col * p : chunk * k + col * (p + 1)] = mixed[p, k]
    await_bytes(mixed.at[:, pl.ds(0, NZ - 1), pl.ds(0, htoks), :], os_.at[0])
    await_bytes(mixed.at[:, :, pl.ds(0, htoks), :], gs.at[0])


def on_device(tokens, norm_gain, expert_ids, gates, gate_proj, up_proj, down_proj):
    toks, features = tokens.shape
    experts = lax.axis_size("expert")
    width = gate_proj.shape[2]
    half, chunk = features // 2, features // NZ
    fine, col = half // (2 * PARTS), chunk // PIECES
    rows = experts * SLOTS
    hrows = rows // 2
    dma = pltpu.SemaphoreType.DMA
    vmem = pl.BlockSpec(memory_space=pltpu.VMEM)
    hbm = pl.BlockSpec(memory_space=pl.ANY)
    b = BATCHES
    scratch = [
        pltpu.VMEM((2, half, width), BF),
        pltpu.VMEM((2, half, width), BF),
        pltpu.VMEM((2, width, half), BF),
        pltpu.VMEM((2, PARTS, SIDE, toks, fine), BF),
        pltpu.VMEM((2, SIDE, experts, toks), F32),
        pltpu.VMEM((b, toks, rows), BF),
        pltpu.VMEM((b, toks, rows), BF),
        pltpu.VMEM((b, 2, SIDE, SIDE, SLOTS, half // 2), BF),
        pltpu.VMEM((b, 2, rows, half), BF),
        pltpu.VMEM((rows, width), F32),
        pltpu.VMEM((rows, width), F32),
        pltpu.VMEM((b, 2, rows, half), BF),
        pltpu.VMEM((b, 2, hrows, half), BF),
        pltpu.VMEM((CHAINS, 4, hrows, chunk), BF),
        pltpu.VMEM((CHAINS, 4, hrows, chunk), BF),
        pltpu.VMEM((CHAINS, 3, hrows, chunk), BF),
        pltpu.VMEM((CHAINS, 3, hrows, chunk), BF),
        pltpu.VMEM((CHAINS, hrows, chunk), BF),
        pltpu.VMEM((CHAINS, rows, chunk), BF),
        pltpu.VMEM((b - CHAINS, NZ // 2, 2, hrows, chunk), BF),
        pltpu.VMEM((b - CHAINS, NZ // 2, rows, chunk), BF),
        pltpu.VMEM((NZ // 2, toks, chunk), BF),
        pltpu.VMEM((NZ, toks // 2, chunk), BF),
        pltpu.VMEM((toks, chunk), F32),
        pltpu.VMEM((PIECES, NZ, toks, col), BF),
        dma((5,)),
        dma((1,)), dma((2, PARTS)),
        dma((1,)), dma((2,)),
        dma((1,)), dma((b,)),
        dma((1,)), dma((b,)),
        dma((1,)), dma((b, 2)),
        dma((1,)), dma((CHAINS, 4)),
        dma((1,)), dma((CHAINS, 3)),
        dma((b,)), dma((CHAINS,)), dma((b - CHAINS, NZ // 2)),
        dma((1,)), dma((1,)),
        dma((1,)), dma((PIECES,)),
        dma((1,)), dma((PIECES,)),
    ]
    return pl.pallas_call(
        kernel,
        out_shape=pltpu.VMEM((toks, features), BF),
        in_specs=[vmem, vmem, vmem, vmem, hbm, hbm, hbm],
        out_specs=vmem,
        scratch_shapes=scratch,
        compiler_params=pltpu.CompilerParams(
            collective_id=0, has_side_effects=True, vmem_limit_bytes=60 << 20
        ),
    )(tokens, norm_gain.reshape(1, -1), expert_ids.T, gates.T, gate_proj, up_proj, down_proj)


def solution(mesh):
    return jax.shard_map(
        on_device,
        mesh=mesh,
        in_specs=(
            P("expert", None),
            P(),
            P("expert", None),
            P("expert", None),
            P("expert", None, "section"),
            P("expert", None, "section"),
            P("expert", "section", None),
        ),
        out_specs=P("expert", None),
        check_vma=False,
    )
```

time: 95.2 us -> 85.2 us (0.89)
  Pallas kernels: 94.2 us -> 84.2 us
    pallas_call x1, Pallas kernels: 94.2 us -> 84.2 us  [on_device(): pl.pallas_call(kernel, out_shape=pltpu.VMEM((toks, features), BF), in_spe...]
where the time goes in v3:
time: 85.2 us; the launch traced here: 85.1 us
  Pallas kernels  84.2 us (99%)
  local copies, waits for them, and re-layouts  0.88 us (1%)
    pallas_call x1, Pallas kernels, on_device(): pl.pallas_call(kernel, out_shape=pltpu.VMEM((toks, features), BF), in_spe...  84.2 us

profile of v3, /device:TPU:1, one launch (start us, length us, event | category | flops | bytes accessed | tf_op | source)
XLA Modules:
  0.0 85.1 jit_solution(7571599614901094603)
XLA Ops:
  0.0 84.2 %shard_map.73 = bf16[128,3072]{1,0:T(8,128)(2,1)S(1)} custom-call(bf16[128,3072]{1,0:T(8,128)(2,1)} %tok.1, f32[1,3072]{1,0:T(1,128)} %bitcast.3, s32[4,128]{1,0:T(4,128)} %bitcast.4, f32[4,128]{1,0:T(4,128)} %bitcast.5, bf16[1,3072,512]{2,1,0:T(8,128)(2,1)} %wg_hbm.1, bf16[1,3072,512]{2,1,0:T(8,128)(2,1)} %wu_hbm.1, bf16[1,512,3072]{2,1,0:T(8,128)(2,1)} %wd_hbm.1), custom_call_target="tpu_custom_call" | custom-call | tf_op jit(solution)/shard_map/pallas_call | solution.py:494
  84.2 0.9 %copy.9 = bf16[128,3072]{1,0:T(8,128)(2,1)} copy(bf16[128,3072]{1,0:T(8,128)(2,1)S(1)} %shard_map.73) | data formatting | bytes 1572864

commit v4 on v3

--- a/solution.py
+++ b/solution.py
@@ -7,12 +7,14 @@
 
 MESH = pl.DeviceIdType.MESH
 BATCHES = 4
-CHAINS = 2
+CHAINS = (0, 2)
+LATE = (1, 3)
 SLOTS = 16
 NZ = 8
 SIDE = 4
 XY = [(dx, dy) for dx in range(SIDE) for dy in range(SIDE) if (dx, dy) != (0, 0)]
-ORDER = ((4, 3, 5, 2), (6, 1, 7, 0))
+ORDER = ((4, 3, 5, 0), (2, 6, 1, 7))
+STAGES = ((0, 3), (3, 4))
 PLACE = {k: (g, i) for g, ks in enumerate(ORDER) for i, k in enumerate(ks)}
 PIECES = 3
 PARTS = 2
@@ -21,10 +23,10 @@
 
 
 def kernel(
-    tok, gain, ids, gates, wg_hbm, wu_hbm, wd_hbm, out,
-    wg, wu, wd, line, slots, chi, clo, packed, xin, gacc, uacc, part, sib,
-    asend, arecv, bsend, brecv, ret_out, ret, late_out, late_in, zsend, zrecv, acc, mixed,
-    w_sem, ls, lr, ns, nr, xs, xr, fs, fr, ps, pr, as_, ar, bs, br, rs, rr, rl, zs, zr, os_, or_, gs, gr,
+    tok_hbm, gain, ids, gates, wg_hbm, wu_hbm, wd_hbm, out,
+    tok, wg, wu, wd, line, slots, chi, clo, packed, xin, gacc, uacc, part, sib,
+    asend, arecv, bsend, brecv, ret_out, ret, late_out, late_in, zsend, zrecv, relay, acc, mixed,
+    w_sem, ls, lr, ns, nr, xs, xr, fs, fr, ps, pr, as_, ar, bs, br, rs, rr, rl, zs, zr, zq, os_, or_, gs, gr,
 ):
     sec, me = lax.axis_index("section"), lax.axis_index("expert")
     z, c = sec // 2, sec % 2
@@ -56,6 +58,9 @@
     other = z * 2 + 1 - c
     sibling = (other, me)
 
+    token_load = pltpu.make_async_copy(tok_hbm, tok, w_sem.at[5])
+    token_load.start()
+
     barrier = pltpu.get_barrier_semaphore()
     for dx, dy in XY:
         for s in (sec, other):
@@ -95,18 +100,17 @@
         slots[f, first_at[f]] = slot
 
     with jax.named_scope("norm"):
+        token_load.wait()
         values = tok[...].astype(F32)
         average = jnp.mean(values, axis=-1, keepdims=True)
         centered = values - average
         variance = jnp.mean(centered * centered, axis=-1, keepdims=True)
-        normed = (centered * lax.rsqrt(variance + 1e-05) * gain[...]).astype(BF)
-        for cc in range(2):
-            @pl.when(c == cc)
-            def _():
-                for f in range(2):
-                    for s in range(PARTS):
-                        at = half * cc + wide * f + fine * s
-                        line[f, s, first_at[f]] = normed[:, at : at + fine]
+        scale = lax.rsqrt(variance + 1e-05)
+        for f in range(2):
+            for s in range(PARTS):
+                cols = pl.ds(pl.multiple_of(half * c + wide * f + fine * s, fine), fine)
+                part_values = tok[:, cols].astype(F32) - average
+                line[f, s, first_at[f]] = (part_values * scale * gain[:, cols]).astype(BF)
 
     def remote(src, dst, send_sem, recv_sem, to):
         return pltpu.make_async_remote_copy(
@@ -210,35 +214,35 @@
         cols = slice(chunk * i + first, chunk * i + first + count)
         return part[j, g, own_rows, cols].astype(F32) + sib[j, g, :, cols].astype(F32)
 
-    def sign(j):
-        return 1 - 2 * (j % 2)
-
-    def chain_a(j, t):
-        return remote(asend.at[j, t], arecv.at[j, t], as_.at[0], ar.at[j, t], zdev(-sign(j)))
-
-    def chain_b(j, t):
-        return remote(bsend.at[j, t], brecv.at[j, t], bs.at[0], br.at[j, t], zdev(sign(j)))
+    def sign(u):
+        return 1 - 2 * (u % 2)
+
+    def chain_a(u, t, p):
+        return remote(asend.at[u, t, p], arecv.at[u, t, p], as_.at[0], ar.at[u, t, p], zdev(-sign(u)))
+
+    def chain_b(u, t, p):
+        return remote(bsend.at[u, t, p], brecv.at[u, t, p], bs.at[0], br.at[u, t, p], zdev(sign(u)))
 
     @jax.named_scope("chain_step")
-    def chain_step(j, t):
-        if j < 0 or j >= CHAINS:
-            return
-        ka, kb = 4 + sign(j) * t, 4 - sign(j) * (1 + t)
+    def chain_step(u, t):
+        j = CHAINS[u]
+        ka, kb = 4 + sign(u) * t, 4 - sign(u) * (1 + t)
         if t < 2:
             sib_p(j, t).wait_recv()
-        total = own_sum(j, ka, 0, chunk)
-        if t > 0:
-            chain_a(j, t - 1).wait_recv()
-            total = total + arecv[j, t - 1].astype(F32)
-        asend[j, t] = total.astype(BF)
-        chain_a(j, t).start()
-        if t < 3:
-            total = own_sum(j, kb, 0, chunk)
+        for p in range(PIECES):
+            total = own_sum(j, ka, col * p, col)
             if t > 0:
-                chain_b(j, t - 1).wait_recv()
-                total = total + brecv[j, t - 1].astype(F32)
-            bsend[j, t] = total.astype(BF)
-            chain_b(j, t).start()
+                chain_a(u, t - 1, p).wait_recv()
+                total = total + arecv[u, t - 1, p].astype(F32)
+            asend[u, t, p] = total.astype(BF)
+            chain_a(u, t, p).start()
+            if t < 3:
+                total = own_sum(j, kb, col * p, col)
+                if t > 0:
+                    chain_b(u, t - 1, p).wait_recv()
+                    total = total + brecv[u, t - 1, p].astype(F32)
+                bsend[u, t, p] = total.astype(BF)
+                chain_b(u, t, p).start()
 
     mine = pl.ds(pl.multiple_of(SLOTS * me, SLOTS), SLOTS)
 
@@ -269,72 +273,107 @@
             await_bytes(ref, sem)
 
     @jax.named_scope("chain_end")
-    def chain_end(j):
-        chain_a(j, 3).wait_recv()
-        chain_b(j, 2).wait_recv()
-        total = own_sum(j, 0, 0, chunk) + arecv[j, 3].astype(F32) + brecv[j, 2].astype(F32)
-        ret_out[j] = total.astype(BF)
-        give_back([ret_out.at[j]] * 2, ret.at[j], rs.at[j], rr.at[j])
+    def chain_end(u):
+        for p in range(PIECES):
+            chain_a(u, 3, p).wait_recv()
+            chain_b(u, 2, p).wait_recv()
+            total = own_sum(CHAINS[u], 0, col * p, col) + arecv[u, 3, p].astype(F32) + brecv[u, 2, p].astype(F32)
+            ret_out[u, :, col * p : col * (p + 1)] = total.astype(BF)
+        give_back([ret_out.at[u]] * 2, ret.at[u], rs.at[CHAINS[u]], rr.at[u])
 
     @jax.named_scope("late_back")
-    def late_back(j):
-        n = j - CHAINS
+    def late_back(n):
+        j = LATE[n]
         for g in range(2):
             sib_p(j, g).wait_recv()
-            total = (part[j, g, own_rows, :].astype(F32) + sib[j, g].astype(F32)).astype(BF)
-            for i in range(NZ // 2):
-                late_out[n, i, g] = total[:, chunk * i : chunk * (i + 1)]
-        for i in range(NZ // 2):
-            give_back([late_out.at[n, i, 0], late_out.at[n, i, 1]], late_in.at[n, i], rs.at[j], rl.at[n, i])
+            for h, (i0, i1) in enumerate(STAGES):
+                cols = slice(chunk * i0, chunk * i1)
+                total = part[j, g, own_rows, cols].astype(F32) + sib[j, g, :, cols].astype(F32)
+                late_out[n, g, :, cols] = total.astype(BF)
+        for h, (i0, i1) in enumerate(STAGES):
+            cols = pl.ds(chunk * i0, chunk * (i1 - i0))
+            give_back(
+                [late_out.at[n, g, :, cols] for g in range(2)], late_in.at[n, :, cols], rs.at[j], rl.at[n, h])
 
     own_toks = pl.ds(pl.multiple_of(htoks * c, htoks), htoks)
 
     @jax.named_scope("mix")
-    def mix(j):
-        await_rows(ret.at[j], rr.at[j])
-        term = jnp.dot(chi[j], ret[j], preferred_element_type=F32)
-        term = term + jnp.dot(clo[j], ret[j], preferred_element_type=F32)
-        acc[...] = term if j == 0 else acc[...] + term
-
-    def give(p, k):
-        here = mixed.at[p, z, own_toks, :]
-        return remote(here, here, os_.at[0], or_.at[p], zdev(k))
+    def mix(u):
+        await_rows(ret.at[u], rr.at[u])
+        term = jnp.dot(chi[CHAINS[u]], ret[u], preferred_element_type=F32)
+        term = term + jnp.dot(clo[CHAINS[u]], ret[u], preferred_element_type=F32)
+        acc[...] = term if u == 0 else acc[...] + term
+
+    def give(p, at, k, first, count, sem):
+        here = mixed.at[p, lax.rem(z + at + NZ, NZ), pl.ds(pl.multiple_of(htoks * c, htoks) + first, count), :]
+        return remote(here, here, os_.at[0], or_.at[p, sem], zdev(k))
+
+    def pass_on(p):
+        for side in (1, -1):
+            await_bytes(mixed.at[p, 0, pl.ds(0, htoks), :], or_.at[p, (1 - side) // 2])
+            give(p, -2 * side, side, 0, htoks, 2).start()
+            give(p, -2 * side, 2 * side, htoks // 4 * (1 - side), htoks // 2, 2).start()
 
     def hand(p):
         here = mixed.at[p, :, own_toks, :]
         return remote(here, here, gs.at[0], gr.at[p], sibling)
 
     @jax.named_scope("late_mix")
-    def late_mix(i):
-        term = jnp.zeros((toks, chunk), F32)
-        for n in range(BATCHES - CHAINS):
-            await_rows(late_in.at[n, i], rl.at[n, i])
-            term = term + jnp.dot(chi[CHAINS + n], late_in[n, i], preferred_element_type=F32)
-            term = term + jnp.dot(clo[CHAINS + n], late_in[n, i], preferred_element_type=F32)
-        zsend[i] = term.astype(BF)
-        k = ORDER[0][i] * (1 - c) + ORDER[1][i] * c
+    def late_mix(h):
+        i0, i1 = STAGES[h]
+        cols = slice(chunk * i0, chunk * i1)
+        term = jnp.zeros((toks, chunk * (i1 - i0)), F32)
+        for n, j in enumerate(LATE):
+            await_rows(late_in.at[n, :, pl.ds(chunk * i0, chunk * (i1 - i0))], rl.at[n, h])
+            term = term + jnp.dot(chi[j], late_in[n, :, cols], preferred_element_type=F32)
+            term = term + jnp.dot(clo[j], late_in[n, :, cols], preferred_element_type=F32)
+        for i in range(i0, i1):
+            zsend[i] = term[:, chunk * (i - i0) : chunk * (i - i0 + 1)].astype(BF)
+        low, high = pl.ds(0, htoks), pl.ds(htoks, htoks)
+
+        @pl.when(c == 0)
+        def _():
+            if h == 0:
+                relay_send(zsend.at[0, low, :], 0, pl.ds(toks, htoks), 2)
+                relay_send(zsend.at[0, high, :], 1, pl.ds(toks, htoks), -2)
+                relay_send(zsend.at[1], 0, pl.ds(0, toks), 1)
+                relay_send(zsend.at[2], 1, pl.ds(0, toks), -1)
+            else:
+                zrecv[0] = zsend[3, :htoks, :]
+                remote(zsend.at[3, high, :], zrecv.at[0], zs.at[0], zr.at[0], sibling).start()
+
+        @pl.when(c == 1)
+        def _():
+            owner_send(2 + h, 1 + h, 1 - 2 * h)
+
+    def relay_send(src, side, rows, k):
+        remote(src, relay.at[side, rows, :], zs.at[0], zq.at[0], zdev(k, 1)).start()
+
+    def owner_send(i, n, k):
         for core in range(2):
-            copy = remote(
-                zsend.at[i, pl.ds(htoks * core, htoks), :], zrecv.at[k], zs.at[0], zr.at[0], zdev(k, core))
-            if ORDER[1][i] == 0 and core == 1:
-                @pl.when(c == 0)
-                def _():
-                    copy.start()
-
-                @pl.when(c == 1)
-                def _():
-                    zrecv[0] = zsend[i, htoks:, :]
-            else:
-                copy.start()
+            remote(zsend.at[i, pl.ds(htoks * core, htoks), :], zrecv.at[n], zs.at[0], zr.at[0], zdev(k, core)).start()
+
+    @jax.named_scope("relay_sum")
+    def relay_sum():
+        @pl.when(c == 1)
+        def _():
+            await_bytes(relay, zq.at[0])
+            for side in range(2):
+                total = zsend[side].astype(F32) + relay[side, :toks, :].astype(F32)
+                far = slice(htoks * side, htoks * (side + 1))
+                near = slice(htoks * (1 - side), htoks * (2 - side))
+                zsend[side, near, :] = total[near, :].astype(BF)
+                zsend[side, far, :] = (total[far, :] + relay[side, toks:, :].astype(F32)).astype(BF)
+                owner_send(side, 3 + side, 2 - 4 * side)
 
     def await_parts(ref, sem):
+        @pl.when(c == 1)
+        def _():
+            await_bytes(ref, sem)
+
         @pl.when(c == 0)
         def _():
-            await_bytes(ref, sem)
-
-        @pl.when(c == 1)
-        def _():
-            await_bytes(ref.at[pl.ds(0, NZ - 1)], sem)
+            await_bytes(ref.at[pl.ds(0, 4)], sem)
 
     @jax.named_scope("gather")
     def gather():
@@ -342,11 +381,11 @@
         for p in range(PIECES):
             cols = slice(col * p, col * (p + 1))
             total = acc[own_toks, cols]
-            for k in range(NZ):
+            for k in range(5):
                 total = total + zrecv[k, :, cols].astype(F32)
             mixed[p, z, own_toks, :] = total.astype(BF)
-            for k in (4, 3, 5, 2, 6, 1, 7):
-                give(p, k).start()
+            for k in (2, -2, 1, -1):
+                give(p, 0, k, 0, htoks, {2: 0, -2: 1, 1: 2, -1: 2}[k]).start()
 
     @jax.named_scope("take")
     def take(j):
@@ -376,12 +415,17 @@
             sib_p(j, g).start()
 
     def after(j):
-        if j < 0:
-            return
-        if j >= CHAINS:
-            late_back(j)
-        for t in range(4):
-            chain_step(j - t, t)
+        if j == 0:
+            chain_step(0, 0)
+        if j == 1:
+            late_back(0)
+            chain_step(0, 1)
+        if j == 2:
+            chain_step(1, 0)
+        if j == 3:
+            chain_step(0, 2)
+            chain_step(1, 1)
+            late_back(1)
 
     take(0)
     for j in range(BATCHES):
@@ -398,16 +442,20 @@
         hidden = up(j, 1)
         if j == 0:
             await_bytes(wd, w_sem.at[4])
-        take(j + 1)
+        if j > 0:
+            take(j + 1)
         down(j, hidden)
+        if j == 0:
+            take(1)
     after(BATCHES - 1)
+    chain_step(1, 2)
+    chain_step(0, 3)
     chain_step(1, 3)
-    chain_end(0)
     late_mix(0)
     chain_end(1)
+    chain_end(0)
     late_mix(1)
-    late_mix(2)
-    late_mix(3)
+    relay_sum()
     mix(0)
     mix(1)
     gather()
@@ -420,16 +468,24 @@
         await_bytes(part.at[:, :, pl.ds(0, hrows), :], ps.at[0])
         await_bytes(asend, as_.at[0])
         await_bytes(bsend, bs.at[0])
-        for j in range(CHAINS):
-            await_rows(ret.at[j], rs.at[j])
-        for n in range(BATCHES - CHAINS):
-            for i in range(NZ // 2):
-                await_rows(late_in.at[n, i], rs.at[CHAINS + n])
-        await_parts(zrecv, zs.at[0])
-
+        for u, j in enumerate(CHAINS):
+            await_rows(ret.at[u], rs.at[j])
+        for n, j in enumerate(LATE):
+            await_rows(late_in.at[n], rs.at[j])
+        @pl.when(c == 0)
+        def _():
+            await_bytes(late_in.at[0, pl.ds(0, 7 * htoks * chunk // half), :], zs.at[0])
+
+        @pl.when(c == 1)
+        def _():
+            await_bytes(zsend, zs.at[0])
+
+    for p in range(PIECES):
+        with jax.named_scope("pass_on"):
+            pass_on(p)
     for p in range(PIECES):
         with jax.named_scope("gather_wait"):
-            await_bytes(mixed.at[p, pl.ds(0, NZ - 1), pl.ds(0, htoks), :], or_.at[p])
+            await_bytes(mixed.at[p, pl.ds(0, NZ - 3), pl.ds(0, htoks), :], or_.at[p, 2])
         hand(p).start()
     for p in range(PIECES):
         with jax.named_scope("hand_wait"):
@@ -453,6 +509,7 @@
     hbm = pl.BlockSpec(memory_space=pl.ANY)
     b = BATCHES
     scratch = [
+        pltpu.VMEM((toks, features), BF),
         pltpu.VMEM((2, half, width), BF),
         pltpu.VMEM((2, half, width), BF),
         pltpu.VMEM((2, width, half), BF),
@@ -466,35 +523,36 @@
         pltpu.VMEM((rows, width), F32),
         pltpu.VMEM((b, 2, rows, half), BF),
         pltpu.VMEM((b, 2, hrows, half), BF),
-        pltpu.VMEM((CHAINS, 4, hrows, chunk), BF),
-        pltpu.VMEM((CHAINS, 4, hrows, chunk), BF),
-        pltpu.VMEM((CHAINS, 3, hrows, chunk), BF),
-        pltpu.VMEM((CHAINS, 3, hrows, chunk), BF),
-        pltpu.VMEM((CHAINS, hrows, chunk), BF),
-        pltpu.VMEM((CHAINS, rows, chunk), BF),
-        pltpu.VMEM((b - CHAINS, NZ // 2, 2, hrows, chunk), BF),
-        pltpu.VMEM((b - CHAINS, NZ // 2, rows, chunk), BF),
+        pltpu.VMEM((len(CHAINS), 4, PIECES, hrows, col), BF),
+        pltpu.VMEM((len(CHAINS), 4, PIECES, hrows, col), BF),
+        pltpu.VMEM((len(CHAINS), 3, PIECES, hrows, col), BF),
+        pltpu.VMEM((len(CHAINS), 3, PIECES, hrows, col), BF),
+        pltpu.VMEM((len(CHAINS), hrows, chunk), BF),
+        pltpu.VMEM((len(CHAINS), rows, chunk), BF),
+        pltpu.VMEM((len(LATE), 2, hrows, half), BF),
+        pltpu.VMEM((len(LATE), rows, half), BF),
         pltpu.VMEM((NZ // 2, toks, chunk), BF),
-        pltpu.VMEM((NZ, toks // 2, chunk), BF),
+        pltpu.VMEM((5, toks // 2, chunk), BF),
+        pltpu.VMEM((2, toks + toks // 2, chunk), BF),
         pltpu.VMEM((toks, chunk), F32),
         pltpu.VMEM((PIECES, NZ, toks, col), BF),
-        dma((5,)),
+        dma((6,)),
         dma((1,)), dma((2, PARTS)),
         dma((1,)), dma((2,)),
         dma((1,)), dma((b,)),
         dma((1,)), dma((b,)),
         dma((1,)), dma((b, 2)),
-        dma((1,)), dma((CHAINS, 4)),
-        dma((1,)), dma((CHAINS, 3)),
-        dma((b,)), dma((CHAINS,)), dma((b - CHAINS, NZ // 2)),
-        dma((1,)), dma((1,)),
-        dma((1,)), dma((PIECES,)),
+        dma((1,)), dma((len(CHAINS), 4, PIECES)),
+        dma((1,)), dma((len(CHAINS), 3, PIECES)),
+        dma((b,)), dma((len(CHAINS),)), dma((len(LATE), len(STAGES))),
+        dma((1,)), dma((1,)), dma((1,)),
+        dma((1,)), dma((PIECES, 3)),
         dma((1,)), dma((PIECES,)),
     ]
     return pl.pallas_call(
         kernel,
         out_shape=pltpu.VMEM((toks, features), BF),
-        in_specs=[vmem, vmem, vmem, vmem, hbm, hbm, hbm],
+        in_specs=[hbm, vmem, vmem, vmem, hbm, hbm, hbm],
         out_specs=vmem,
         scratch_shapes=scratch,
         compiler_params=pltpu.CompilerParams(

time: 85.2 us -> 81.6 us (0.958)
  Pallas kernels: 84.2 us -> 80.6 us
    pallas_call x1, Pallas kernels: 84.2 us -> 80.6 us  [on_device(): pl.pallas_call(kernel, out_shape=pltpu.VMEM((toks, features), BF), in_spe...]
where the time goes in v4:
time: 81.6 us; the launch traced here: 81.5 us
  Pallas kernels  80.6 us (99%)
  local copies, waits for them, and re-layouts  0.88 us (1%)
    pallas_call x1, Pallas kernels, on_device(): pl.pallas_call(kernel, out_shape=pltpu.VMEM((toks, features), BF), in_spe...  80.6 us

profile of v4, /device:TPU:1, one launch (start us, length us, event | category | flops | bytes accessed | tf_op | source)
XLA Modules:
  0.0 81.5 jit_solution(9436132922987734986)
XLA Ops:
  0.0 80.6 %shard_map.73 = bf16[128,3072]{1,0:T(8,128)(2,1)S(1)} custom-call(bf16[128,3072]{1,0:T(8,128)(2,1)} %tok_hbm.1, f32[1,3072]{1,0:T(1,128)} %bitcast.3, s32[4,128]{1,0:T(4,128)} %bitcast.4, f32[4,128]{1,0:T(4,128)} %bitcast.5, bf16[1,3072,512]{2,1,0:T(8,128)(2,1)} %wg_hbm.1, bf16[1,3072,512]{2,1,0:T(8,128)(2,1)} %wu_hbm.1, bf16[1,512,3072]{2,1,0:T(8,128)(2,1)} %wd_hbm.1), custom_call_target="tpu_custom_call" | custom-call | tf_op jit(solution)/shard_map/pallas_call | solution.py:552
  80.6 0.9 %copy.9 = bf16[128,3072]{1,0:T(8,128)(2,1)} copy(bf16[128,3072]{1,0:T(8,128)(2,1)S(1)} %shard_map.73) | data formatting | bytes 1572864

commit v5 on v4

--- a/solution.py
+++ b/solution.py
@@ -413,6 +413,8 @@
         for g in range(2):
             part[j, g] = jnp.dot(hidden, wd[g], preferred_element_type=F32).astype(BF)
             sib_p(j, g).start()
+            if j == 0 and g == 0:
+                take(1)
 
     def after(j):
         if j == 0:
@@ -433,20 +435,21 @@
             loads[0].wait()
             loads[1].wait()
         up(j, 0)
-        after(j - 1)
+        if j != 2:
+            after(j - 1)
         if j == 0:
             loads[2].wait()
             loads[3].wait()
         with jax.named_scope("sib_wait"):
             sib_x(j).wait_recv()
         hidden = up(j, 1)
+        if j == 2:
+            after(1)
         if j == 0:
             await_bytes(wd, w_sem.at[4])
         if j > 0:
             take(j + 1)
         down(j, hidden)
-        if j == 0:
-            take(1)
     after(BATCHES - 1)
     chain_step(1, 2)
     chain_step(0, 3)

time: 81.6 us -> 80.2 us (0.983)
  Pallas kernels: 80.6 us -> 79.1 us
    pallas_call x1, Pallas kernels: 80.6 us -> 79.1 us  [on_device(): pl.pallas_call(kernel, out_shape=pltpu.VMEM((toks, features), BF), in_spe...]
where the time goes in v5:
time: 80.2 us; the launch traced here: 80 us
  Pallas kernels  79.1 us (99%)
  local copies, waits for them, and re-layouts  0.88 us (1%)
    pallas_call x1, Pallas kernels, on_device(): pl.pallas_call(kernel, out_shape=pltpu.VMEM((toks, features), BF), in_spe...  79.1 us

profile of v5, /device:TPU:1, one launch (start us, length us, event | category | flops | bytes accessed | tf_op | source)
XLA Modules:
  0.0 80.0 jit_solution(14152542345854350565)
XLA Ops:
  0.0 79.1 %shard_map.73 = bf16[128,3072]{1,0:T(8,128)(2,1)S(1)} custom-call(bf16[128,3072]{1,0:T(8,128)(2,1)} %tok_hbm.1, f32[1,3072]{1,0:T(1,128)} %bitcast.3, s32[4,128]{1,0:T(4,128)} %bitcast.4, f32[4,128]{1,0:T(4,128)} %bitcast.5, bf16[1,3072,512]{2,1,0:T(8,128)(2,1)} %wg_hbm.1, bf16[1,3072,512]{2,1,0:T(8,128)(2,1)} %wu_hbm.1, bf16[1,512,3072]{2,1,0:T(8,128)(2,1)} %wd_hbm.1), custom_call_target="tpu_custom_call" | custom-call | tf_op jit(solution)/shard_map/pallas_call | solution.py:555
  79.1 0.9 %copy.9 = bf16[128,3072]{1,0:T(8,128)(2,1)} copy(bf16[128,3072]{1,0:T(8,128)(2,1)S(1)} %shard_map.73) | data formatting | bytes 1572864

commit v6 on v5

--- a/solution.py
+++ b/solution.py
@@ -17,7 +17,7 @@
 STAGES = ((0, 3), (3, 4))
 PLACE = {k: (g, i) for g, ks in enumerate(ORDER) for i, k in enumerate(ks)}
 PIECES = 3
-PARTS = 2
+PARTS = 3
 BF = jnp.bfloat16
 F32 = jnp.float32
 
@@ -451,8 +451,8 @@
             take(j + 1)
         down(j, hidden)
     after(BATCHES - 1)
+    chain_step(0, 3)
     chain_step(1, 2)
-    chain_step(0, 3)
     chain_step(1, 3)
     late_mix(0)
     chain_end(1)

time: 80.2 us -> 80.2 us (level)
  no operation moved by 1% of the time
where the time goes in v6:
time: 80.2 us; the launch traced here: 80.1 us
  Pallas kernels  79.2 us (99%)
  local copies, waits for them, and re-layouts  0.88 us (1%)
    pallas_call x1, Pallas kernels, on_device(): pl.pallas_call(kernel, out_shape=pltpu.VMEM((toks, features), BF), in_spe...  79.2 us

profile of v6, /device:TPU:1, one launch (start us, length us, event | category | flops | bytes accessed | tf_op | source)
XLA Modules:
  0.0 80.1 jit_solution(2645122713843115073)
XLA Ops:
  0.0 79.2 %shard_map.73 = bf16[128,3072]{1,0:T(8,128)(2,1)S(1)} custom-call(bf16[128,3072]{1,0:T(8,128)(2,1)} %tok_hbm.1, f32[1,3072]{1,0:T(1,128)} %bitcast.3, s32[4,128]{1,0:T(4,128)} %bitcast.4, f32[4,128]{1,0:T(4,128)} %bitcast.5, bf16[1,3072,512]{2,1,0:T(8,128)(2,1)} %wg_hbm.1, bf16[1,3072,512]{2,1,0:T(8,128)(2,1)} %wu_hbm.1, bf16[1,512,3072]{2,1,0:T(8,128)(2,1)} %wd_hbm.1), custom_call_target="tpu_custom_call" | custom-call | tf_op jit(solution)/shard_map/pallas_call | solution.py:555
  79.2 0.9 %copy.9 = bf16[128,3072]{1,0:T(8,128)(2,1)} copy(bf16[128,3072]{1,0:T(8,128)(2,1)S(1)} %shard_map.73) | data formatting | bytes 1572864
